TPU v7x, 32 devices: a whole 2x2x4 slice. The times are simulated.
32 devices in a mesh: sub: 4 (over x, core), lat: 4 (over z), lon: 2 (over y).
Axes of the slice: x: 2, y: 2, z: 4, core: 2. Of those that a mesh axis runs over, the one named last changes fastest.
Arguments:
- increment: float32 [4, 64, 128, 512], P('sub', 'lat', 'lon'), may hold values from -6 to 6
- multiplier: float32 [4, 64, 128, 512], P('sub', 'lat', 'lon'), may hold values from -6 to 6
- background: bfloat16 [4, 64, 128, 512], P('sub', 'lat', 'lon'), may hold values from -6 to 6
- obs_cotangent: bfloat16 [4, 8, 2048, 512], P('sub', ('lat', 'lon')), may hold values from -6 to 6
- obs_column: int32 [4, 8, 2048], P('sub', ('lat', 'lon')), may hold values from 0 to 1023
- obs_count: int32 [4, 8], P('sub'), may hold values from 1 to 2048, 8192 in all within a row
- transport: float32 [8, 512], replicated, may hold values from 0.015 to 0.1
- hidden_weight: bfloat16 [512, 1024], replicated, may hold values from -0.25 to 0.25
- hidden_bias: float32 [1024], replicated, may hold values from -3 to 3
- output_weight: bfloat16 [1024, 512], replicated, may hold values from -0.1875 to 0.1875
Outputs:
- model_error: float32 [4, 64, 128, 512], P('sub', 'lat', 'lon')
- gradient: float32 [4, 64, 128, 512], P('sub', 'lat', 'lon')
- obs_tangent: bfloat16 [4, 8, 2048, 512], P('sub', ('lat', 'lon'))
Inputs may be any that keep to these rules, and one draw needn't show every extreme that they name: `obs_count`: the counts of one subwindow sum to 8192, and one of them equals 2048. `obs_column`: slots at or beyond their block's count are unused.
All inputs are finite; a program needn't handle non-finite values.
Results may differ from a plain program's by a relative error of at most 0.0058.
Values may be sent and summed in bfloat16 or wider, within the bound.
A program may use at most 128 MiB of HBM per device.

v0:
```python
import jax
import jax.numpy as jnp
from jax import lax
from jax.sharding import PartitionSpec as P

STEPS = 4


def padded_2(cells, sides, width):
    for axis, dim in sides:
        count = lax.axis_size(axis)
        ends = count - 1
        head = lax.slice_in_dim(cells, 0, width, axis=dim)
        tail = lax.slice_in_dim(cells, cells.shape[dim] - width, cells.shape[dim], axis=dim)
        cells = jnp.concatenate(
            [
                lax.ppermute(tail, axis, [(i, (i + 1) % count) for i in range(ends)]),
                cells,
                lax.ppermute(head, axis, [((i + 1) % count, i) for i in range(ends)]),
            ],
            axis=dim,
        )
    return cells


def shifted(array, axis, by):
    count = lax.axis_size(axis)
    pairs = [(i, i + by) for i in range(count) if 0 <= i + by < count]
    return lax.ppermute(array, axis, pairs)


def observe(state_rows, back_rows, cot_rows, hidden_weight, hidden_bias, output_weight):
    preact = jnp.dot(back_rows, hidden_weight, preferred_element_type=jnp.float32) + hidden_bias
    hidden = jnp.tanh(preact)
    slopes = 1.0 - hidden * hidden
    forward = jnp.dot(state_rows, hidden_weight, preferred_element_type=jnp.float32)
    scaled = (slopes * forward).astype(jnp.bfloat16)
    tangent = jnp.dot(scaled, output_weight, preferred_element_type=jnp.float32).astype(
        jnp.bfloat16
    )
    pulled = jnp.dot(cot_rows, output_weight.T, preferred_element_type=jnp.float32)
    weighted = (slopes * pulled).astype(jnp.bfloat16)
    adjoint = jnp.dot(weighted, hidden_weight.T, preferred_element_type=jnp.float32).astype(
        jnp.bfloat16
    )
    return (tangent, adjoint)


def mirrored(transport):
    return jnp.stack(
        [
            transport[3],
            transport[2],
            transport[1],
            transport[0],
            transport[7],
            transport[6],
            transport[5],
            transport[4],
        ]
    )


def advance(window, coeffs):
    total_rate = jnp.sum(coeffs, axis=1)[:, None, None, :]
    rate_terms = [coeffs[:, offset_index][:, None, None, :] for offset_index in range(8)]
    height = window.shape[1]
    across = window.shape[2]
    for sweep_step in range(STEPS):
        padded = padded_2(window.astype(jnp.bfloat16), (("lat", 1), ("lon", 2)), 2).astype(
            window.dtype
        )
        window = (
            (1.0 - total_rate) * window
            + rate_terms[0] * padded[:, 0:height, 2 : across + 2]
            + rate_terms[1] * padded[:, 1 : height + 1, 2 : across + 2]
            + rate_terms[2] * padded[:, 3 : height + 3, 2 : across + 2]
            + rate_terms[3] * padded[:, 4 : height + 4, 2 : across + 2]
            + rate_terms[4] * padded[:, 2 : height + 2, 0:across]
            + rate_terms[5] * padded[:, 2 : height + 2, 1 : across + 1]
            + rate_terms[6] * padded[:, 2 : height + 2, 3 : across + 3]
            + rate_terms[7] * padded[:, 2 : height + 2, 4 : across + 4]
        )
    return window


def local(
    increment,
    multiplier,
    background,
    obs_cotangent,
    obs_column,
    obs_count,
    transport,
    hidden_weight,
    hidden_bias,
    output_weight,
):
    reverse_rates = mirrored(transport)
    joined = advance(
        jnp.concatenate([increment, multiplier], axis=0), jnp.stack([transport, reverse_rates])
    )
    ahead = joined[0:1]
    behind = joined[1:2]
    carried = shifted(ahead.astype(jnp.bfloat16), "sub", 1).astype(ahead.dtype)
    returned = shifted(behind.astype(jnp.bfloat16), "sub", -1).astype(behind.dtype)
    model_error = increment - carried
    obs_slots = obs_column.shape[2]
    counts_row = obs_count[0]
    myself = lax.axis_index(("lat", "lon"))
    my_count = counts_row[myself]
    alive_rows = (jnp.arange(obs_slots, dtype=jnp.int32) < my_count)[:, None]
    columns = obs_column[0, 0]
    levels = increment.shape[3]
    state_rows = jnp.take(increment[0].reshape(-1, levels), columns, axis=0).astype(jnp.bfloat16)
    back_rows = jnp.take(background[0].reshape(-1, levels), columns, axis=0)
    cot_rows = obs_cotangent[0, 0]
    tangent, adjoint = observe(
        state_rows, back_rows, cot_rows, hidden_weight, hidden_bias, output_weight
    )
    tangent = jnp.where(alive_rows, tangent, jnp.zeros_like(tangent))
    adjoint_wide = jnp.where(alive_rows, adjoint.astype(jnp.float32), jnp.zeros((), jnp.float32))
    column_total = increment.shape[1] * increment.shape[2]
    obs_adjoint = (
        jnp.zeros((column_total, levels), jnp.float32)
        .at[columns]
        .add(adjoint_wide)
        .reshape(increment.shape)
    )
    gradient = multiplier - returned + obs_adjoint
    return (model_error, gradient, tangent[None, None])


def solution(mesh):
    in_specs = (
        P("sub", "lat", "lon", None),
        P("sub", "lat", "lon", None),
        P("sub", "lat", "lon", None),
        P("sub", ("lat", "lon"), None, None),
        P("sub", ("lat", "lon"), None),
        P("sub", None),
        P(),
        P(),
        P(),
        P(),
    )
    out_specs = (
        P("sub", "lat", "lon", None),
        P("sub", "lat", "lon", None),
        P("sub", ("lat", "lon"), None, None),
    )
    return jax.shard_map(local, mesh=mesh, in_specs=in_specs, out_specs=out_specs, check_vma=False)
```

profile of v0, /device:TPU:1, one launch (start us, length us, event | category | flops | bytes accessed | tf_op | source)
XLA Modules:
  0.0 210.0 jit_solution(14627146638922094888)
XLA Ops:
  0.7 2.0 constant_dynamic-update-slice_fusion.1
  3.2 1.9 copy-done.2
  6.9 4.0 %collective-permute-start = (bf16[2,2,64,512]{3,2,1,0:T(8,128)(2,1)S(1)}, bf16[2,2,64,512]{3,2,1,0:T(8,128)(2,1)S(1)}, u32[]{:S(2)}, u32[]{:S(2)}) collective-permute-start(bf16[2,2,64,512]{3,2,1,0:T(8,128)(2,1)S(1)} %get-tuple-element.25), channel_id=1, source_target_pairs={{0,2},{2,4},{4,6},{1,3},{3,5},{5,7},{8,10},{10,12},{12,14},{9,11},... | collective-permute-start | bytes 786440 | tf_op jit(solution)/shard_map/ppermute | solution.py:17
  12.4 3.4 %collective-permute-done = bf16[2,2,64,512]{3,2,1,0:T(8,128)(2,1)S(1)} collective-permute-done((bf16[2,2,64,512]{3,2,1,0:T(8,128)(2,1)S(1)}, bf16[2,2,64,512]{3,2,1,0:T(8,128)(2,1)S(1)}, u32[]{:S(2)}, u32[]{:S(2)}) %collective-permute-start) | collective-permute-done | bytes 262176 | tf_op jit(solution)/shard_map/ppermute | solution.py:17
  15.9 3.8 %collective-permute-done.1 = bf16[2,2,64,512]{3,2,1,0:T(8,128)(2,1)S(1)} collective-permute-done((bf16[2,2,64,512]{3,2,1,0:T(8,128)(2,1)S(1)}, bf16[2,2,64,512]{3,2,1,0:T(8,128)(2,1)S(1)}, u32[]{:S(2)}, u32[]{:S(2)}) %collective-permute-start.1) | collective-permute-done | bytes 262176 | tf_op jit(solution)/shard_map/ppermute | solution.py:19
  20.9 3.1 %collective-permute-start.2 = (bf16[2,20,2,512]{3,2,1,0:T(2,128)(2,1)S(1)}, bf16[2,20,2,512]{3,2,1,0:T(2,128)(2,1)S(1)}, u32[]{:S(2)}, u32[]{:S(2)}) collective-permute-start(bf16[2,20,2,512]{3,2,1,0:T(2,128)(2,1)S(1)} %get-tuple-element.15), channel_id=1, source_target_pairs={{0,1},{2,3},{4,5},{6,7},{8,9},{10,11},{12,13},{14,15},{16,17},{18,... | collective-permute-start | bytes 245768 | tf_op jit(solution)/shard_map/ppermute | solution.py:17
  25.6 3.7 %collective-permute-done.3 = bf16[2,20,2,512]{3,2,1,0:T(2,128)(2,1)S(1)} collective-permute-done((bf16[2,20,2,512]{3,2,1,0:T(2,128)(2,1)S(1)}, bf16[2,20,2,512]{3,2,1,0:T(2,128)(2,1)S(1)}, u32[]{:S(2)}, u32[]{:S(2)}) %collective-permute-start.3) | collective-permute-done | bytes 81952 | tf_op jit(solution)/shard_map/ppermute | solution.py:19
  29.3 2.2 %maximum_convert_fusion = f32[2,20,68,512]{3,2,1,0:T(8,128)S(1)} fusion(bf16[2,20,2,512]{3,2,1,0:T(2,128)(2,1)S(1)} %collective-permute-done.3, bf16[2,2,64,512]{3,2,1,0:T(8,128)(2,1)} %copy-done.10, bf16[2,16,64,512]{3,2,1,0:T(8,128)(2,1)S(1)} %copy-done.4, bf16[2,2,64,512]{3,2,1,0:T(8,128)(2,1)S(1)} %collective-permute-done, ...), kind=kLoop, calls=%fused_computation.77 | loop fusion | flops 13926400 | bytes 8355840 | tf_op jit(solution)/shard_map/convert_element_type | solution.py:70
  31.5 9.9 %fusion.68 = (bf16[2,16,64,512]{3,2,1,0:T(8,128)(2,1)}, f32[2,16,64,512]{3,2,1,0:T(8,128)}) fusion(f32[2,20,68,512]{3,2,1,0:T(8,128)S(1)} %maximum_convert_fusion, f32[2,512]{1,0:T(2,128)S(1)} %get-tuple-element.43, f32[2,512]{1,0:T(2,128)S(1)} %get-tuple-element.44, f32[2,512]{1,0:T(2,128)S(1)} %get-tuple-element.45, f32[2,512]{1,0:T(2,128)S(1)} %get-tuple-element.46, ...), kind=kLoop, calls=%fused_computation.156 | loop fusion | flops 18874368 | bytes 44077056 | tf_op jit(solution)/shard_map/convert_element_type | solution.py:70
  42.6 3.2 %collective-permute-start.4 = (bf16[2,2,64,512]{3,2,1,0:T(8,128)(2,1)S(1)}, bf16[2,2,64,512]{3,2,1,0:T(8,128)(2,1)S(1)}, u32[]{:S(2)}, u32[]{:S(2)}) collective-permute-start(bf16[2,2,64,512]{3,2,1,0:T(8,128)(2,1)S(1)} %get-tuple-element.23), channel_id=1, source_target_pairs={{0,2},{2,4},{4,6},{1,3},{3,5},{5,7},{8,10},{10,12},{12,14},{9,11},... | collective-permute-start | bytes 786440 | tf_op jit(solution)/shard_map/ppermute | solution.py:17
  47.1 2.0 collective-permute-done.4
  49.1 3.8 %collective-permute-done.5 = bf16[2,2,64,512]{3,2,1,0:T(8,128)(2,1)S(1)} collective-permute-done((bf16[2,2,64,512]{3,2,1,0:T(8,128)(2,1)S(1)}, bf16[2,2,64,512]{3,2,1,0:T(8,128)(2,1)S(1)}, u32[]{:S(2)}, u32[]{:S(2)}) %collective-permute-start.5) | collective-permute-done | bytes 262176 | tf_op jit(solution)/shard_map/ppermute | solution.py:19
  57.1 3.7 %collective-permute-done.7 = bf16[2,20,2,512]{3,2,1,0:T(2,128)(2,1)S(1)} collective-permute-done((bf16[2,20,2,512]{3,2,1,0:T(2,128)(2,1)S(1)}, bf16[2,20,2,512]{3,2,1,0:T(2,128)(2,1)S(1)}, u32[]{:S(2)}, u32[]{:S(2)}) %collective-permute-start.7) | collective-permute-done | bytes 81952 | tf_op jit(solution)/shard_map/ppermute | solution.py:19
  62.1 9.9 %fusion.66 = (bf16[2,16,64,512]{3,2,1,0:T(8,128)(2,1)}, f32[2,16,64,512]{3,2,1,0:T(8,128)}) fusion(f32[2,20,68,512]{3,2,1,0:T(8,128)S(1)} %maximum_convert_fusion.1, f32[2,512]{1,0:T(2,128)S(1)} %get-tuple-element.43, f32[2,512]{1,0:T(2,128)S(1)} %get-tuple-element.44, f32[2,512]{1,0:T(2,128)S(1)} %get-tuple-element.45, f32[2,512]{1,0:T(2,128)S(1)} %get-tuple-element.46, ...), kind=kLoop, calls=%fused_computation.155 | loop fusion | flops 18874368 | bytes 44077056 | tf_op jit(solution)/shard_map/convert_element_type | solution.py:70
  74.0 3.5 %collective-permute-start.8 = (bf16[2,2,64,512]{3,2,1,0:T(8,128)(2,1)}, bf16[2,2,64,512]{3,2,1,0:T(8,128)(2,1)S(1)}, u32[]{:S(2)}, u32[]{:S(2)}) collective-permute-start(bf16[2,2,64,512]{3,2,1,0:T(8,128)(2,1)} %get-tuple-element.21), channel_id=1, source_target_pairs={{0,2},{2,4},{4,6},{1,3},{3,5},{5,7},{8,10},{10,12},{12,14},{9,11},... | collective-permute-start | bytes 786440 | tf_op jit(solution)/shard_map/ppermute | solution.py:17
  81.1 3.8 %collective-permute-done.9 = bf16[2,2,64,512]{3,2,1,0:T(8,128)(2,1)} collective-permute-done((bf16[2,2,64,512]{3,2,1,0:T(8,128)(2,1)}, bf16[2,2,64,512]{3,2,1,0:T(8,128)(2,1)}, u32[]{:S(2)}, u32[]{:S(2)}) %collective-permute-start.9) | collective-permute-done | bytes 262176 | tf_op jit(solution)/shard_map/ppermute | solution.py:19
  91.0 9.2 %gather_fusion = bf16[2048,512]{1,0:T(8,128)(2,1)} fusion(bf16[1024,512]{1,0:T(8,128)(2,1)S(1)} %bitcast.38, s32[2048]{0:T(1024)S(1)} %broadcast_clamp_fusion), kind=kCustom, calls=%fused_computation | custom fusion | bytes 4202496 | tf_op jit(solution)/shard_map/jit(_take)/gather | solution.py:116
  100.9 2.5 %maximum_convert_fusion.2 = f32[2,20,68,512]{3,2,1,0:T(8,128)S(1)} fusion(bf16[2,20,2,512]{3,2,1,0:T(2,128)(2,1)} %collective-permute-done.11, bf16[2,2,64,512]{3,2,1,0:T(8,128)(2,1)} %collective-permute-done.9, bf16[2,16,64,512]{3,2,1,0:T(8,128)(2,1)} %get-tuple-element.5, bf16[2,2,64,512]{3,2,1,0:T(8,128)(2,1)S(1)} %collective-permute-done.8, ...), kind=kLoop, calls=%fused_computation.79 | loop fusion | flops 13926400 | bytes 8355840 | tf_op jit(solution)/shard_map/convert_element_type | solution.py:70
  103.4 9.9 %fusion.64 = (bf16[2,16,64,512]{3,2,1,0:T(8,128)(2,1)}, f32[2,16,64,512]{3,2,1,0:T(8,128)}) fusion(f32[2,20,68,512]{3,2,1,0:T(8,128)S(1)} %maximum_convert_fusion.2, f32[2,512]{1,0:T(2,128)S(1)} %get-tuple-element.43, f32[2,512]{1,0:T(2,128)S(1)} %get-tuple-element.44, f32[2,512]{1,0:T(2,128)S(1)} %get-tuple-element.45, f32[2,512]{1,0:T(2,128)S(1)} %get-tuple-element.46, ...), kind=kLoop, calls=%fused_computation.154 | loop fusion | flops 18874368 | bytes 44077056 | tf_op jit(solution)/shard_map/convert_element_type | solution.py:70
  117.6 7.7 %fusion.41 = f32[2048,1024]{1,0:T(8,128)} fusion(bf16[512,1024]{1,0:T(8,128)(2,1)} %param.17, bf16[2048,512]{1,0:T(8,128)(2,1)} %gather_fusion, pred[2048]{0:T(1024)(128)(4,1)S(1)} %copy-done.15), kind=kOutput, calls=%fused_computation.86 | convolution fusion | flops 2148532224 | bytes 11536384 | tf_op jit(solution)/shard_map/dot_general | solution.py:33
  125.5 4.4 %collective-permute-start.14 = (bf16[2,20,2,512]{3,2,1,0:T(2,128)(2,1)S(1)}, bf16[2,20,2,512]{3,2,1,0:T(2,128)(2,1)S(1)}, u32[]{:S(2)}, u32[]{:S(2)}) collective-permute-start(bf16[2,20,2,512]{3,2,1,0:T(2,128)(2,1)S(1)} %get-tuple-element.9), channel_id=1, source_target_pairs={{0,1},{2,3},{4,5},{6,7},{8,9},{10,11},{12,13},{14,15},{16,17},{18,... | collective-permute-start | bytes 245768 | tf_op jit(solution)/shard_map/ppermute | solution.py:17
  131.4 9.9 %convolution_convert_fusion.1 = bf16[2048,512]{1,0:T(8,128)(2,1)} fusion(bf16[512,1024]{1,0:T(8,128)(2,1)} %param.17, f32[2048,1024]{1,0:T(8,128)} %fusion.41, bf16[1024,512]{1,0:T(8,128)(2,1)} %param.19, f32[1024]{0:T(1024)S(1)} %copy-done.16, bf16[1,1,2048,512]{3,2,1,0:T(8,128)(2,1)S(1)} %copy-done), kind=kOutput, calls=%fused_computation.76 | convolution fusion | flops 4306501632 | bytes 14684160 | tf_op jit(solution)/shard_map/dot_general | solution.py:43
  141.3 10.8 %gather_fusion.1 = bf16[2048,512]{1,0:T(8,128)(2,1)} fusion(f32[1024,512]{1,0:T(8,128)} %bitcast.39, s32[2048]{0:T(1024)S(1)} %broadcast_clamp_fusion), kind=kCustom, calls=%fused_computation.1 | custom fusion | bytes 4202496 | tf_op jit(solution)/shard_map/jit(_take)/gather | solution.py:115
  152.2 15.7 %scatter_custom_fusion = f32[1024,512]{1,0:T(8,128)} fusion(s32[2048]{0:T(1024)} %bitcast.47, bf16[2048,512]{1,0:T(8,128)(2,1)} %convolution_convert_fusion.1, f32[]{:T(128)} %constant.17.clone.1, pred[2048]{0:T(1024)(128)(4,1)S(1)} %get-tuple-element.51), kind=kCustom, calls=%fused_computation.72 | custom fusion | flops 3145728 | bytes 4197376 | tf_op jit(solution)/shard_map/scatter-add | solution.py:127
  167.9 2.4 %maximum_convert_fusion.3 = f32[2,20,68,512]{3,2,1,0:T(8,128)S(1)} fusion(bf16[2,20,2,512]{3,2,1,0:T(2,128)(2,1)S(1)} %collective-permute-done.15, bf16[2,2,64,512]{3,2,1,0:T(8,128)(2,1)S(1)} %collective-permute-done.13, bf16[2,16,64,512]{3,2,1,0:T(8,128)(2,1)} %get-tuple-element.3, bf16[2,2,64,512]{3,2,1,0:T(8,128)(2,1)S(1)} %collective-permute-done.12, ...), kind=kLoop, calls=%fused_computation.80 | loop fusion | flops 13926400 | bytes 8355840 | tf_op jit(solution)/shard_map/convert_element_type | solution.py:70
  170.3 8.2 %fusion.1 = bf16[2,16,64,512]{3,2,1,0:T(8,128)(2,1)S(1)} fusion(f32[2,20,68,512]{3,2,1,0:T(8,128)S(1)} %maximum_convert_fusion.3, f32[2,16,64,512]{3,2,1,0:T(8,128)} %get-tuple-element.4, f32[2,512]{1,0:T(2,128)S(1)} %get-tuple-element.43, f32[2,512]{1,0:T(2,128)S(1)} %get-tuple-element.44, f32[2,512]{1,0:T(2,128)S(1)} %get-tuple-element.45, ...), kind=kLoop, calls=%fused_computation.8 | loop fusion | flops 18874368 | bytes 39882752 | tf_op jit(solution)/shard_map/convert.1
  180.0 9.4 %collective-permute-start.17 = (bf16[1,16,64,512]{3,2,1,0:T(8,128)(2,1)}, bf16[1,16,64,512]{3,2,1,0:T(8,128)(2,1)S(1)}, u32[]{:S(2)}, u32[]{:S(2)}) collective-permute-start(bf16[1,16,64,512]{3,2,1,0:T(8,128)(2,1)} %get-tuple-element.17), channel_id=1, source_target_pairs={{8,0},{16,8},{24,16},{9,1},{17,9},{25,17},{10,2},{18,10},{26,18},{... | collective-permute-start | bytes 3145736 | tf_op jit(solution)/shard_map/ppermute | solution.py:29
  189.4 3.0 %collective-permute-start.16 = (bf16[1,16,64,512]{3,2,1,0:T(8,128)(2,1)}, bf16[1,16,64,512]{3,2,1,0:T(8,128)(2,1)}, u32[]{:S(2)}, u32[]{:S(2)}) collective-permute-start(bf16[1,16,64,512]{3,2,1,0:T(8,128)(2,1)} %get-tuple-element.18), channel_id=1, source_target_pairs={{0,8},{8,16},{16,24},{1,9},{9,17},{17,25},{2,10},{10,18},{18,26},{... | collective-permute-start | bytes 3145736 | tf_op jit(solution)/shard_map/ppermute | solution.py:29
  192.4 8.9 %fusion.37 = bf16[1,1,2048,512]{3,2,1,0:T(8,128)(2,1)} fusion(bf16[1024,512]{1,0:T(8,128)(2,1)} %param.19, pred[2048]{0:T(1024)(128)(4,1)S(1)} %get-tuple-element.51, f32[2048,1024]{1,0:T(8,128)} %fusion.41, bf16[512,1024]{1,0:T(8,128)(2,1)} %param.17, f32[1024]{0:T(1024)S(1)} %copy-done.16, bf16[2048,512]{1,0:T(8,128)(2,1)} %gather_fusion.1, ...), kind=kOutput, calls=%fused_computation.82 | convolution fusion | flops 4308598784 | bytes 14688256 | tf_op jit(solution)/shard_map/dot_general | solution.py:38
  201.4 3.1 %collective-permute-done.16 = bf16[1,16,64,512]{3,2,1,0:T(8,128)(2,1)} collective-permute-done((bf16[1,16,64,512]{3,2,1,0:T(8,128)(2,1)}, bf16[1,16,64,512]{3,2,1,0:T(8,128)(2,1)}, u32[]{:S(2)}, u32[]{:S(2)}) %collective-permute-start.16) | collective-permute-done | bytes 1048608 | tf_op jit(solution)/shard_map/ppermute | solution.py:29
  204.5 3.5 %convert_subtract_fusion = f32[1,16,64,512]{3,2,1,0:T(8,128)} fusion(f32[1,16,64,512]{3,2,1,0:T(8,128)} %param.10, bf16[1,16,64,512]{3,2,1,0:T(8,128)(2,1)} %collective-permute-done.16), kind=kLoop, calls=%fused_computation.89 | loop fusion | flops 1048576 | bytes 5242880 | tf_op jit(solution)/shard_map/sub | solution.py:107
  208.0 2.0 subtract_add_fusion
  (81 shorter events, 34.0 us)
Async XLA Ops:
  0.6 130.8 %copy-start = (bf16[1,1,2048,512]{3,2,1,0:T(8,128)(2,1)S(1)}, bf16[1,1,2048,512]{3,2,1,0:T(8,128)(2,1)}, u32[]{:S(2)}) copy-start(bf16[1,1,2048,512]{3,2,1,0:T(8,128)(2,1)} %param.13) | copy-start | bytes 6291460
  5.2 7.0 %copy-start.11 = (f32[8,512]{1,0:T(8,128)S(1)}, f32[8,512]{1,0:T(8,128)}, u32[]{:S(2)}) copy-start(f32[8,512]{1,0:T(8,128)} %param.16) | copy-start | bytes 49156
  6.9 9.0 %collective-permute-start = (bf16[2,2,64,512]{3,2,1,0:T(8,128)(2,1)S(1)}, bf16[2,2,64,512]{3,2,1,0:T(8,128)(2,1)S(1)}, u32[]{:S(2)}, u32[]{:S(2)}) collective-permute-start(bf16[2,2,64,512]{3,2,1,0:T(8,128)(2,1)S(1)} %get-tuple-element.25), channel_id=1, source_target_pairs={{0,2},{2,4},{4,6},{1,3},{3,5},{5,7},{8,10},{10,12},{12,14},{9,11},... | collective-permute-start | bytes 786440 | tf_op jit(solution)/shard_map/ppermute | solution.py:17
  10.9 8.8 %collective-permute-start.1 = (bf16[2,2,64,512]{3,2,1,0:T(8,128)(2,1)S(1)}, bf16[2,2,64,512]{3,2,1,0:T(8,128)(2,1)S(1)}, u32[]{:S(2)}, u32[]{:S(2)}) collective-permute-start(bf16[2,2,64,512]{3,2,1,0:T(8,128)(2,1)S(1)} %get-tuple-element.26), channel_id=1, source_target_pairs={{2,0},{4,2},{6,4},{3,1},{5,3},{7,5},{10,8},{12,10},{14,12},{11,9},... | collective-permute-start | bytes 786440 | tf_op jit(solution)/shard_map/ppermute | solution.py:19
  12.3 17.0 %copy-start.4 = (bf16[2,16,64,512]{3,2,1,0:T(8,128)(2,1)S(1)}, bf16[2,16,64,512]{3,2,1,0:T(8,128)(2,1)}, u32[]{:S(2)}) copy-start(bf16[2,16,64,512]{3,2,1,0:T(8,128)(2,1)} %copy-done.3) | copy-start | bytes 6291460
  19.7 5.9 %copy-start.10 = (bf16[2,2,64,512]{3,2,1,0:T(8,128)(2,1)}, bf16[2,2,64,512]{3,2,1,0:T(8,128)(2,1)S(1)}, u32[]{:S(2)}) copy-start(bf16[2,2,64,512]{3,2,1,0:T(8,128)(2,1)S(1)} %collective-permute-done.1) | copy-start | bytes 786436
  20.9 4.6 %collective-permute-start.2 = (bf16[2,20,2,512]{3,2,1,0:T(2,128)(2,1)S(1)}, bf16[2,20,2,512]{3,2,1,0:T(2,128)(2,1)S(1)}, u32[]{:S(2)}, u32[]{:S(2)}) collective-permute-start(bf16[2,20,2,512]{3,2,1,0:T(2,128)(2,1)S(1)} %get-tuple-element.15), channel_id=1, source_target_pairs={{0,1},{2,3},{4,5},{6,7},{8,9},{10,11},{12,13},{14,15},{16,17},{18,... | collective-permute-start | bytes 245768 | tf_op jit(solution)/shard_map/ppermute | solution.py:17
  24.1 5.2 %collective-permute-start.3 = (bf16[2,20,2,512]{3,2,1,0:T(2,128)(2,1)S(1)}, bf16[2,20,2,512]{3,2,1,0:T(2,128)(2,1)S(1)}, u32[]{:S(2)}, u32[]{:S(2)}) collective-permute-start(bf16[2,20,2,512]{3,2,1,0:T(2,128)(2,1)S(1)} %get-tuple-element.16), channel_id=1, source_target_pairs={{1,0},{3,2},{5,4},{7,6},{9,8},{11,10},{13,12},{15,14},{17,16},{19,... | collective-permute-start | bytes 245768 | tf_op jit(solution)/shard_map/ppermute | solution.py:19
  41.4 19.5 %copy-start.6 = (bf16[2,16,64,512]{3,2,1,0:T(8,128)(2,1)S(1)}, bf16[2,16,64,512]{3,2,1,0:T(8,128)(2,1)}, u32[]{:S(2)}) copy-start(bf16[2,16,64,512]{3,2,1,0:T(8,128)(2,1)} %get-tuple-element.7) | copy-start | bytes 6291460
  42.6 6.5 %collective-permute-start.4 = (bf16[2,2,64,512]{3,2,1,0:T(8,128)(2,1)S(1)}, bf16[2,2,64,512]{3,2,1,0:T(8,128)(2,1)S(1)}, u32[]{:S(2)}, u32[]{:S(2)}) collective-permute-start(bf16[2,2,64,512]{3,2,1,0:T(8,128)(2,1)S(1)} %get-tuple-element.23), channel_id=1, source_target_pairs={{0,2},{2,4},{4,6},{1,3},{3,5},{5,7},{8,10},{10,12},{12,14},{9,11},... | collective-permute-start | bytes 786440 | tf_op jit(solution)/shard_map/ppermute | solution.py:17
  45.8 7.1 %collective-permute-start.5 = (bf16[2,2,64,512]{3,2,1,0:T(8,128)(2,1)S(1)}, bf16[2,2,64,512]{3,2,1,0:T(8,128)(2,1)S(1)}, u32[]{:S(2)}, u32[]{:S(2)}) collective-permute-start(bf16[2,2,64,512]{3,2,1,0:T(8,128)(2,1)S(1)} %get-tuple-element.24), channel_id=1, source_target_pairs={{2,0},{4,2},{6,4},{3,1},{5,3},{7,5},{10,8},{12,10},{14,12},{11,9},... | collective-permute-start | bytes 786440 | tf_op jit(solution)/shard_map/ppermute | solution.py:19
  54.1 3.0 %collective-permute-start.6 = (bf16[2,20,2,512]{3,2,1,0:T(2,128)(2,1)S(1)}, bf16[2,20,2,512]{3,2,1,0:T(2,128)(2,1)S(1)}, u32[]{:S(2)}, u32[]{:S(2)}) collective-permute-start(bf16[2,20,2,512]{3,2,1,0:T(2,128)(2,1)S(1)} %get-tuple-element.13), channel_id=1, source_target_pairs={{0,1},{2,3},{4,5},{6,7},{8,9},{10,11},{12,13},{14,15},{16,17},{18,... | collective-permute-start | bytes 245768 | tf_op jit(solution)/shard_map/ppermute | solution.py:17
  55.6 5.2 %collective-permute-start.7 = (bf16[2,20,2,512]{3,2,1,0:T(2,128)(2,1)S(1)}, bf16[2,20,2,512]{3,2,1,0:T(2,128)(2,1)S(1)}, u32[]{:S(2)}, u32[]{:S(2)}) collective-permute-start(bf16[2,20,2,512]{3,2,1,0:T(2,128)(2,1)S(1)} %get-tuple-element.14), channel_id=1, source_target_pairs={{1,0},{3,2},{5,4},{7,6},{9,8},{11,10},{13,12},{15,14},{17,16},{19,... | collective-permute-start | bytes 245768 | tf_op jit(solution)/shard_map/ppermute | solution.py:19
  62.1 16.7 %copy-start.13 = (s32[1,1,2048]{2,1,0:T(1,128)S(1)}, s32[1,1,2048]{2,1,0:T(1,128)}, u32[]{:S(2)}) copy-start(s32[1,1,2048]{2,1,0:T(1,128)} %param.14) | copy-start | bytes 24580
  62.1 16.7 %copy-start.17 = (s32[1,8]{1,0:T(1,128)S(1)}, s32[1,8]{1,0:T(1,128)}, u32[]{:S(2)}) copy-start(s32[1,8]{1,0:T(1,128)} %param.15) | copy-start | bytes 100
  72.0 19.0 %copy-start.1 = (bf16[1,16,64,512]{3,2,1,0:T(8,128)(2,1)S(1)}, bf16[1,16,64,512]{3,2,1,0:T(8,128)(2,1)}, u32[]{:S(2)}) copy-start(bf16[1,16,64,512]{3,2,1,0:T(8,128)(2,1)} %param.12) | copy-start | bytes 3145732
  74.0 7.1 %collective-permute-start.8 = (bf16[2,2,64,512]{3,2,1,0:T(8,128)(2,1)}, bf16[2,2,64,512]{3,2,1,0:T(8,128)(2,1)S(1)}, u32[]{:S(2)}, u32[]{:S(2)}) collective-permute-start(bf16[2,2,64,512]{3,2,1,0:T(8,128)(2,1)} %get-tuple-element.21), channel_id=1, source_target_pairs={{0,2},{2,4},{4,6},{1,3},{3,5},{5,7},{8,10},{10,12},{12,14},{9,11},... | collective-permute-start | bytes 786440 | tf_op jit(solution)/shard_map/ppermute | solution.py:17
  77.5 7.4 %collective-permute-start.9 = (bf16[2,2,64,512]{3,2,1,0:T(8,128)(2,1)}, bf16[2,2,64,512]{3,2,1,0:T(8,128)(2,1)}, u32[]{:S(2)}, u32[]{:S(2)}) collective-permute-start(bf16[2,2,64,512]{3,2,1,0:T(8,128)(2,1)} %get-tuple-element.22), channel_id=1, source_target_pairs={{2,0},{4,2},{6,4},{3,1},{5,3},{7,5},{10,8},{12,10},{14,12},{11,9},... | collective-permute-start | bytes 786440 | tf_op jit(solution)/shard_map/ppermute | solution.py:19
  78.8 8.0 %copy-start.14 = (s32[2048,1]{0,1:T(1,128)}, s32[2048,1]{0,1:T(1,128)S(1)}, u32[]{:S(2)}) copy-start(s32[2048,1]{0,1:T(1,128)S(1)} %compare_select_fusion) | copy-start | bytes 24580
  86.8 13.5 %collective-permute-start.10 = (bf16[2,20,2,512]{3,2,1,0:T(2,128)(2,1)}, bf16[2,20,2,512]{3,2,1,0:T(2,128)(2,1)S(1)}, u32[]{:S(2)}, u32[]{:S(2)}) collective-permute-start(bf16[2,20,2,512]{3,2,1,0:T(2,128)(2,1)} %get-tuple-element.11), channel_id=1, source_target_pairs={{0,1},{2,3},{4,5},{6,7},{8,9},{10,11},{12,13},{14,15},{16,17},{18,... | collective-permute-start | bytes 245768 | tf_op jit(solution)/shard_map/ppermute | solution.py:17
  88.3 12.5 %collective-permute-start.11 = (bf16[2,20,2,512]{3,2,1,0:T(2,128)(2,1)}, bf16[2,20,2,512]{3,2,1,0:T(2,128)(2,1)}, u32[]{:S(2)}, u32[]{:S(2)}) collective-permute-start(bf16[2,20,2,512]{3,2,1,0:T(2,128)(2,1)} %get-tuple-element.12), channel_id=1, source_target_pairs={{1,0},{3,2},{5,4},{7,6},{9,8},{11,10},{13,12},{15,14},{17,16},{19,... | collective-permute-start | bytes 245768 | tf_op jit(solution)/shard_map/ppermute | solution.py:19
  103.4 14.2 %copy-start.15 = (pred[2048]{0:T(1024)(128)(4,1)S(1)}, pred[2048]{0:T(1024)(128)(4,1)}, u32[]{:S(2)}) copy-start(pred[2048]{0:T(1024)(128)(4,1)} %get-tuple-element.52) | copy-start | bytes 6148
  114.3 11.0 %collective-permute-start.12 = (bf16[2,2,64,512]{3,2,1,0:T(8,128)(2,1)S(1)}, bf16[2,2,64,512]{3,2,1,0:T(8,128)(2,1)S(1)}, u32[]{:S(2)}, u32[]{:S(2)}) collective-permute-start(bf16[2,2,64,512]{3,2,1,0:T(8,128)(2,1)S(1)} %get-tuple-element.19), channel_id=1, source_target_pairs={{0,2},{2,4},{4,6},{1,3},{3,5},{5,7},{8,10},{10,12},{12,14},{9,11},... | collective-permute-start | bytes 786440 | tf_op jit(solution)/shard_map/ppermute | solution.py:17
  116.3 9.0 %collective-permute-start.13 = (bf16[2,2,64,512]{3,2,1,0:T(8,128)(2,1)S(1)}, bf16[2,2,64,512]{3,2,1,0:T(8,128)(2,1)S(1)}, u32[]{:S(2)}, u32[]{:S(2)}) collective-permute-start(bf16[2,2,64,512]{3,2,1,0:T(8,128)(2,1)S(1)} %get-tuple-element.20), channel_id=1, source_target_pairs={{2,0},{4,2},{6,4},{3,1},{5,3},{7,5},{10,8},{12,10},{14,12},{11,9},... | collective-permute-start | bytes 786440 | tf_op jit(solution)/shard_map/ppermute | solution.py:19
  117.6 7.7 %copy-start.5 = (bf16[2,16,64,512]{3,2,1,0:T(8,128)(2,1)S(1)}, bf16[2,16,64,512]{3,2,1,0:T(8,128)(2,1)}, u32[]{:S(2)}) copy-start(bf16[2,16,64,512]{3,2,1,0:T(8,128)(2,1)} %get-tuple-element.3) | copy-start | bytes 6291460
  117.6 13.8 %copy-start.16 = (f32[1024]{0:T(1024)S(1)}, f32[1024]{0:T(1024)}, u32[]{:S(2)}) copy-start(f32[1024]{0:T(1024)} %param.18) | copy-start | bytes 12292
  125.5 42.4 %collective-permute-start.14 = (bf16[2,20,2,512]{3,2,1,0:T(2,128)(2,1)S(1)}, bf16[2,20,2,512]{3,2,1,0:T(2,128)(2,1)S(1)}, u32[]{:S(2)}, u32[]{:S(2)}) collective-permute-start(bf16[2,20,2,512]{3,2,1,0:T(2,128)(2,1)S(1)} %get-tuple-element.9), channel_id=1, source_target_pairs={{0,1},{2,3},{4,5},{6,7},{8,9},{10,11},{12,13},{14,15},{16,17},{18,... | collective-permute-start | bytes 245768 | tf_op jit(solution)/shard_map/ppermute | solution.py:17
  129.9 38.0 %collective-permute-start.15 = (bf16[2,20,2,512]{3,2,1,0:T(2,128)(2,1)S(1)}, bf16[2,20,2,512]{3,2,1,0:T(2,128)(2,1)S(1)}, u32[]{:S(2)}, u32[]{:S(2)}) collective-permute-start(bf16[2,20,2,512]{3,2,1,0:T(2,128)(2,1)S(1)} %get-tuple-element.10), channel_id=1, source_target_pairs={{1,0},{3,2},{5,4},{7,6},{9,8},{11,10},{13,12},{15,14},{17,16},{19,... | collective-permute-start | bytes 245768 | tf_op jit(solution)/shard_map/ppermute | solution.py:19
  180.0 28.0 %collective-permute-start.17 = (bf16[1,16,64,512]{3,2,1,0:T(8,128)(2,1)}, bf16[1,16,64,512]{3,2,1,0:T(8,128)(2,1)S(1)}, u32[]{:S(2)}, u32[]{:S(2)}) collective-permute-start(bf16[1,16,64,512]{3,2,1,0:T(8,128)(2,1)} %get-tuple-element.17), channel_id=1, source_target_pairs={{8,0},{16,8},{24,16},{9,1},{17,9},{25,17},{10,2},{18,10},{26,18},{... | collective-permute-start | bytes 3145736 | tf_op jit(solution)/shard_map/ppermute | solution.py:29
  189.4 15.1 %collective-permute-start.16 = (bf16[1,16,64,512]{3,2,1,0:T(8,128)(2,1)}, bf16[1,16,64,512]{3,2,1,0:T(8,128)(2,1)}, u32[]{:S(2)}, u32[]{:S(2)}) collective-permute-start(bf16[1,16,64,512]{3,2,1,0:T(8,128)(2,1)} %get-tuple-element.18), channel_id=1, source_target_pairs={{0,8},{8,16},{16,24},{1,9},{9,17},{17,25},{2,10},{10,18},{18,26},{... | collective-permute-start | bytes 3145736 | tf_op jit(solution)/shard_map/ppermute | solution.py:29
  201.4 6.7 %copy-start.8 = (f32[1,16,64,512]{3,2,1,0:T(8,128)S(1)}, f32[1,16,64,512]{3,2,1,0:T(8,128)}, u32[]{:S(2)}) copy-start(f32[1,16,64,512]{3,2,1,0:T(8,128)} %param.11) | copy-start | bytes 6291460
  201.4 6.7 %copy-start.9 = (f32[1024,512]{1,0:T(8,128)S(1)}, f32[1024,512]{1,0:T(8,128)}, u32[]{:S(2)}) copy-start(f32[1024,512]{1,0:T(8,128)} %scatter_custom_fusion) | copy-start | bytes 6291460
  (4 other events, 6.3 us)
where the time goes:
time: 213 us; the launch traced here: 210 us
  other arithmetic  73.5 us (35%)
  starting transfers between devices  46.5 us (22%)
  local copies, waits for them, and re-layouts  33 us (15%)
  waiting for transfers between devices  29.4 us (14%)
  matrix products  26.5 us (12%)
    convert_element_type x4, other arithmetic, advance(): window.astype(jnp.bfloat16)  30 us
    ppermute x8, starting transfers between devices, padded_2(): lax.ppermute(tail, axis, [(i, (i + 1) % count) for i in range(ends)])  23.4 us
    ppermute x8, waiting for transfers between devices, padded_2(): lax.ppermute(head, axis, [((i + 1) % count, i) for i in range(ends)])  18.9 us
    scatter-add x1, other arithmetic, local(): obs_adjoint = jnp.zeros((column_total, levels), jnp.float32).at[columns]....  15.7 us
    ppermute x2, starting transfers between devices, shifted(): return lax.ppermute(array, axis, pairs)  12.4 us
    gather x1, local copies, waits for them, and re-layouts, local(): jnp.take(increment[0].reshape(-1, levels), columns, axis=0)  10.8 us
    ppermute x8, starting transfers between devices, padded_2(): lax.ppermute(head, axis, [((i + 1) % count, i) for i in range(ends)])  10.7 us
    dot_general x1, matrix products, observe(): jnp.dot(weighted, hidden_weight.T, preferred_element_type=jnp.float32)  9.91 us
  transfers between devices with their start and end apart: 18, of which 11 were waited for; matrix products, arithmetic and copies ran while one was open for 32% of the time, Pallas kernels for 0%

commit v1 on v0

v1 whole, which is shorter than its diff:
```python
import functools

import jax
import jax.numpy as jnp
from jax import lax
from jax.experimental import pallas as pl
from jax.experimental.pallas import tpu as pltpu
from jax.sharding import PartitionSpec as P

STEPS = 4
REACH = 2
HALO = STEPS * REACH
SUB = 8
LANES = 128
NT = (((1,), (1,)), ((), ()))
F32 = jnp.float32
BF16 = jnp.bfloat16


def dot(a, b):
    return jnp.dot(a, b, preferred_element_type=F32)


def dot_nt(a, b):
    return lax.dot_general(a, b, NT, preferred_element_type=F32)


def observe_kernel(count_ref, cols_ref, state_ref, back_ref, cot_ref, hw_ref, bias_ref, ow_ref,
                   tangent_ref, adjoint_ref, per_column, slot_cols):
    columns, levels = state_ref.shape
    slots = cot_ref.shape[0]
    count = count_ref[0]
    tile = min(256, columns)
    chunks = slots // LANES
    place = (lax.broadcasted_iota(jnp.int32, (chunks, LANES), 0) * LANES
             + lax.broadcasted_iota(jnp.int32, (chunks, LANES), 1))
    slot_cols[...] = jnp.where(place < count, cols_ref[...], -1)

    @pl.loop(0, columns // tile)
    def _(t):
        base = pl.multiple_of(t * tile, tile)
        rows = pl.ds(base, tile)
        wanted = lax.broadcasted_iota(jnp.int32, (tile, LANES), 0) + base
        hits = [jnp.where(slot_cols[k:k + 1, :] == wanted, 1.0, 0.0).astype(BF16) for k in range(chunks)]
        summed = dot(jnp.concatenate(hits, axis=1), cot_ref[...]).astype(BF16)
        hidden = jnp.tanh(dot(back_ref[rows, :], hw_ref[...]) + bias_ref[...])
        slopes = 1.0 - hidden * hidden
        forward = dot(state_ref[rows, :].astype(BF16), hw_ref[...])
        per_column[rows, :] = dot((slopes * forward).astype(BF16), ow_ref[...]).astype(BF16)
        pulled = dot_nt(summed, ow_ref[...])
        adjoint_ref[rows, :] = dot_nt((slopes * pulled).astype(BF16), hw_ref[...])

    @pl.loop(0, slots // 256)
    def _(t):
        parts = []
        for h in range(2):
            named = jnp.transpose(jnp.broadcast_to(slot_cols[pl.ds(t * 2 + h, 1), :], (LANES, LANES)))
            lane = lax.broadcasted_iota(jnp.int32, (LANES, LANES), 1)
            hits = [jnp.where(named == lane + c * LANES, 1.0, 0.0).astype(BF16) for c in range(columns // LANES)]
            parts.append(jnp.concatenate(hits, axis=1))
        tangent_ref[pl.ds(pl.multiple_of(t * 256, 256), 256), :] = dot(
            jnp.concatenate(parts, axis=0), per_column[...]).astype(BF16)


def observe(count, cols, state, back, cot, hw, bias, ow):
    columns, levels = state.shape
    slots, chan = cot.shape
    hid = hw.shape[1]
    vm = pl.BlockSpec(memory_space=pltpu.VMEM)
    flops = 2 * columns * levels * hid * 5 + 4 * columns * slots * chan
    return pl.pallas_call(
        observe_kernel,
        out_shape=(jax.ShapeDtypeStruct((slots, chan), BF16), jax.ShapeDtypeStruct((columns, levels), F32)),
        in_specs=[pl.BlockSpec(memory_space=pltpu.SMEM)] + [vm] * 7,
        out_specs=(vm, vm),
        scratch_shapes=[pltpu.VMEM((columns, chan), BF16), pltpu.VMEM((slots // LANES, LANES), jnp.int32)],
        compiler_params=pltpu.CompilerParams(vmem_limit_bytes=40 << 20),
        cost_estimate=pl.CostEstimate(flops=flops, bytes_accessed=14 << 20, transcendentals=columns * hid),
        name="observe",
    )(count, cols, state, back, cot, hw, bias, ow)


def transport_field(lat_first, lat_last, lon_first, center, above, below, side, weights, window, state, width, n_lon):
    height = center.shape[0]
    across = center.shape[1]
    total = height + 2 * HALO
    start = jnp.where(lon_first, 0, HALO) if n_lon > 1 else 0
    side_at = jnp.where(lon_first, across, 0)
    if n_lon > 1:
        start = pl.multiple_of(start, HALO)
        side_at = pl.multiple_of(side_at, HALO)
    window[pl.ds(0, HALO), pl.ds(start, across), :] = above[...].astype(F32)
    window[pl.ds(HALO, height), pl.ds(start, across), :] = center[...].astype(F32)
    window[pl.ds(HALO + height, HALO), pl.ds(start, across), :] = below[...].astype(F32)
    if n_lon > 1:
        window[:, pl.ds(side_at, HALO), :] = side[...].astype(F32)

    @pl.loop(0, total)
    def _(r):
        for v in range(width):
            state[0, r, v] = window[r, pl.ds(v, SUB, stride=width), :]

    @pl.when(jnp.logical_or(lat_first, lat_last))
    def _():
        zero = jnp.zeros((HALO, width, SUB, LANES), F32)

        @pl.when(lat_first)
        def _():
            state[1, pl.ds(0, HALO)] = zero

        @pl.when(lat_last)
        def _():
            state[1, pl.ds(HALO + height, HALO)] = zero

    lane_row = lax.broadcasted_iota(jnp.int32, (SUB, LANES), 0)
    low_edge = lane_row == 0
    high_edge = lane_row == SUB - 1
    c = [jnp.broadcast_to(weights[k:k + 1, :], (SUB, LANES)) for k in range(9)]
    for step in range(STEPS):
        src, dst = step % 2, (step + 1) % 2
        lo = REACH * (step + 1)
        first = jnp.where(lat_first, HALO, lo)
        last = jnp.where(lat_last, HALO + height, total - lo)

        @pl.loop(first, last)
        def _(r):
            row = [state[src, r, v] for v in range(width)]
            before = [jnp.where(low_edge, 0.0, pltpu.roll(row[width - REACH + k], 1, 0)) for k in range(REACH)]
            after = [jnp.where(high_edge, 0.0, pltpu.roll(row[k], SUB - 1, 0)) for k in range(REACH)]
            line = before + row + after
            for v in range(width):
                acc = c[8] * row[v]
                acc += c[0] * state[src, r - 2, v]
                acc += c[1] * state[src, r - 1, v]
                acc += c[2] * state[src, r + 1, v]
                acc += c[3] * state[src, r + 2, v]
                acc += c[4] * line[v]
                acc += c[5] * line[v + 1]
                acc += c[6] * line[v + 3]
                acc += c[7] * line[v + 4]
                if step == STEPS - 1:
                    window[r, pl.ds(v, SUB, stride=width), :] = acc
                else:
                    state[dst, r, v] = acc
    return start


def transport_kernel(axes, width, wa_ref, wm_ref, a_mid, a_up, a_down, a_side, m_mid, m_up, m_down, m_side,
                     inc_ref, mul_ref, adj_ref, err_ref, grad_ref, window, state):
    n_lat, n_lon = axes
    lat = lax.axis_index("lat")
    lon = lax.axis_index("lon")
    height, across = a_mid.shape[0], a_mid.shape[1]
    place = (lat == 0, lat == n_lat - 1, lon == 0)
    start = transport_field(*place, a_mid, a_up, a_down, a_side, wa_ref, window, state, width, n_lon)
    err_ref[...] = inc_ref[...] - window[pl.ds(HALO, height), pl.ds(start, across), :]
    start = transport_field(*place, m_mid, m_up, m_down, m_side, wm_ref, window, state, width, n_lon)
    grad_ref[...] = mul_ref[...] - window[pl.ds(HALO, height), pl.ds(start, across), :] + adj_ref[...]


def transport_call(axes, wa, wm, a_parts, m_parts, inc, mul, adj):
    n_lat, n_lon = axes
    height, across, levels = inc.shape
    width = (across + (HALO if n_lon > 1 else 0)) // SUB
    total = height + 2 * HALO
    whole = lambda rows, cols: pl.BlockSpec((rows, cols, LANES), lambda g: (0, 0, g))
    field = [whole(height, across), whole(HALO, across), whole(HALO, across), whole(total, HALO)]
    w_spec = pl.BlockSpec((9, LANES), lambda g: (0, g))
    return pl.pallas_call(
        functools.partial(transport_kernel, axes, width),
        grid=(levels // LANES,),
        out_shape=(jax.ShapeDtypeStruct(inc.shape, F32),) * 2,
        in_specs=[w_spec, w_spec] + field + field + [whole(height, across)] * 3,
        out_specs=(whole(height, across),) * 2,
        scratch_shapes=[
            pltpu.VMEM((total, width * SUB, LANES), F32),
            pltpu.VMEM((2, total, width, SUB, LANES), F32),
        ],
        compiler_params=pltpu.CompilerParams(vmem_limit_bytes=40 << 20),
        cost_estimate=pl.CostEstimate(flops=2 * 4 * 17 * height * across * levels, bytes_accessed=18 << 20, transcendentals=0),
        name="transport",
    )(wa, wm, *a_parts, *m_parts, inc, mul, adj)


def shifted(array, axis, by):
    count = lax.axis_size(axis)
    pairs = [(i, i + by) for i in range(count) if 0 <= i + by < count]
    return lax.ppermute(array, axis, pairs)


def with_halo(mid):
    height, across, levels = mid.shape
    up = shifted(mid[height - HALO:], "lat", 1)
    down = shifted(mid[:HALO], "lat", -1)
    if lax.axis_size("lon") == 1:
        return mid, up, down, jnp.zeros((height + 2 * HALO, HALO, levels), mid.dtype)
    first = lax.axis_index("lon") == 0
    edge = lambda x: lax.dynamic_slice_in_dim(x, jnp.where(first, across - HALO, 0), HALO, axis=1)
    side = lax.ppermute(jnp.concatenate([edge(up), edge(mid), edge(down)], axis=0), "lon", [(0, 1), (1, 0)])
    return mid, up, down, side


def local(increment, multiplier, background, obs_cotangent, obs_column, obs_count, transport,
          hidden_weight, hidden_bias, output_weight):
    n_lat, n_lon = lax.axis_size("lat"), lax.axis_size("lon")
    assert n_lon <= 2
    inc, mul = increment[0], multiplier[0]
    levels = inc.shape[-1]
    rest = (1.0 - jnp.sum(transport, axis=0))[None]
    wa = jnp.concatenate([transport, rest], axis=0)
    wm = jnp.concatenate([transport[3::-1], transport[7:3:-1], rest], axis=0)
    a_parts = with_halo(shifted(inc.astype(BF16), "sub", 1))
    m_parts = with_halo(shifted(mul.astype(BF16), "sub", -1))
    myself = lax.axis_index(("lat", "lon"))
    count = lax.dynamic_slice_in_dim(obs_count[0], myself, 1)
    tangent, adj = observe(count, obs_column.reshape(-1, LANES), inc.reshape(-1, levels),
                           background.reshape(-1, levels), obs_cotangent[0, 0], hidden_weight,
                           hidden_bias[None], output_weight)
    err, grad = transport_call((n_lat, n_lon), wa, wm, a_parts, m_parts, inc, mul, adj.reshape(inc.shape))
    return err[None], grad[None], tangent[None, None]


def solution(mesh):
    field = P("sub", "lat", "lon", None)
    slots = P("sub", ("lat", "lon"), None, None)
    in_specs = (field, field, field, slots, P("sub", ("lat", "lon"), None), P("sub", None), P(), P(), P(), P())
    return jax.shard_map(local, mesh=mesh, in_specs=in_specs, out_specs=(field, field, slots), check_vma=False)
```

time: 213 us -> 136 us (0.64)
  the two profiles are of different devices: /device:TPU:1 before, /device:TPU:13 now
where the time goes in v1:
time: 136 us
  Pallas kernels  79.9 us (59%)
  waiting for transfers between devices  21.5 us (16%)
  starting transfers between devices  17.6 us (13%)
  local copies, waits for them, and re-layouts  11.6 us (9%)
  other arithmetic  4.08 us (3%)
    pallas_call x1, Pallas kernels, transport_call(): pl.pallas_call(functools.partial(transport_kernel, axes, width), grid=(le...  65.1 us
    ppermute x6, starting transfers between devices, shifted(): return lax.ppermute(array, axis, pairs)  17.1 us
    pallas_call x1, Pallas kernels, observe(): pl.pallas_call(observe_kernel, out_shape=(jax.ShapeDtypeStruct((slots, ch...  14.8 us
    ppermute x6, waiting for transfers between devices, shifted(): return lax.ppermute(array, axis, pairs)  13.3 us
    ppermute x2, waiting for transfers between devices, with_halo(): lax.ppermute(jnp.concatenate([edge(up), edge(mid), edge(down)], axis=0),...  8.22 us
    unnamed x26, local copies, waits for them, and re-layouts  6.62 us
    convert_element_type x1, other arithmetic, local(): a_parts = with_halo(shifted(inc.astype(BF16), 'sub', 1))  2.86 us
  transfers between devices with their start and end apart: 8, of which 5 were waited for; matrix products, arithmetic and copies ran while one was open for 5% of the time, Pallas kernels for 11%

profile of v1, /device:TPU:13, one launch (start us, length us, event | category | flops | bytes accessed | tf_op | source)
XLA Modules:
  0.0 135.5 jit_solution(17179851974966610991)
XLA Ops:
  0.6 0.0 copy-start
  0.6 0.0 copy-start.2
  0.7 2.9 %bitcast_convert_fusion.1 = bf16[16,64,512]{2,1,0:T(8,128)(2,1)} fusion(f32[1,16,64,512]{3,2,1,0:T(8,128)} %param.10), kind=kLoop, calls=%fused_computation.13 | loop fusion | flops 524288 | bytes 3145728 | tf_op jit(solution)/shard_map/convert_element_type | solution.py:212
  3.5 3.8 %collective-permute-start = (bf16[16,64,512]{2,1,0:T(8,128)(2,1)}, bf16[16,64,512]{2,1,0:T(8,128)(2,1)S(1)}, u32[]{:S(2)}, u32[]{:S(2)}) collective-permute-start(bf16[16,64,512]{2,1,0:T(8,128)(2,1)} %bitcast_convert_fusion.1), channel_id=1, source_target_pairs={{0,8},{8,16},{16,24},{1,9},{9,17},{17,25},{2,10},{10,18},{18,26},{... | collective-permute-start | bytes 3145736 | tf_op jit(solution)/shard_map/ppermute | solution.py:188
  7.3 1.1 bitcast_convert_fusion
  8.5 1.9 %collective-permute-start.4 = (bf16[16,64,512]{2,1,0:T(8,128)(2,1)}, bf16[16,64,512]{2,1,0:T(8,128)(2,1)}, u32[]{:S(2)}, u32[]{:S(2)}) collective-permute-start(bf16[16,64,512]{2,1,0:T(8,128)(2,1)} %bitcast_convert_fusion), channel_id=1, source_target_pairs={{8,0},{16,8},{24,16},{9,1},{17,9},{25,17},{10,2},{18,10},{26,18},{... | collective-permute-start | bytes 3145736 | tf_op jit(solution)/shard_map/ppermute | solution.py:188
  10.4 0.6 constant_dynamic-slice_fusion
  11.0 1.6 %copy-done.6 = bf16[1,1,2048,512]{3,2,1,0:T(8,128)(2,1)S(1)} copy-done((bf16[1,1,2048,512]{3,2,1,0:T(8,128)(2,1)S(1)}, bf16[1,1,2048,512]{3,2,1,0:T(8,128)(2,1)}, u32[]{:S(2)}) %copy-start.6) | copy-done | bytes 2097176
  12.6 1.2 copy-done.7
  13.8 1.2 copy-done.8
  15.0 1.2 copy-done.9
  16.3 14.8 %observe.1 = (bf16[2048,512]{1,0:T(8,128)(2,1)}, f32[1024,512]{1,0:T(8,128)S(1)}) custom-call(s32[1]{0:T(128)} %bitcast.3.count_ref, s32[16,128]{1,0:T(8,128)S(1)} %bitcast.21, f32[1024,512]{1,0:T(8,128)S(1)} %bitcast.15, bf16[1024,512]{1,0:T(8,128)(2,1)S(1)} %bitcast.20, bf16[2048,512]{1,0:T(8,128)(2,1)S(1)} %bitcast.19, bf16[512,1024]{1,0:T(8,128)(2,1)S(1)} %copy-done.8, ...), custom_call_target="tpu_custom_call" | custom-call | flops 9663676416 | bytes 14680064 | tf_op jit(solution)/shard_map/observe/pallas_call | solution.py:71
  31.0 1.3 copy-done.4
  32.4 1.1 fusion.1
  33.4 2.1 %collective-permute-start.2 = (bf16[8,64,512]{2,1,0:T(8,128)(2,1)}, bf16[8,64,512]{2,1,0:T(8,128)(2,1)}, u32[]{:S(2)}, u32[]{:S(2)}) collective-permute-start(bf16[8,64,512]{2,1,0:T(8,128)(2,1)} %get-tuple-element.13), channel_id=1, source_target_pairs={{2,0},{4,2},{6,4},{3,1},{5,3},{7,5},{10,8},{12,10},{14,12},{11,9},... | collective-permute-start | bytes 1572872 | tf_op jit(solution)/shard_map/ppermute | solution.py:188
  35.6 0.1 rev.6
  35.7 0.1 rev.7
  35.8 0.0 copy-start.3
  35.9 3.5 %collective-permute-start.1 = (bf16[8,64,512]{2,1,0:T(8,128)(2,1)}, bf16[8,64,512]{2,1,0:T(8,128)(2,1)S(1)}, u32[]{:S(2)}, u32[]{:S(2)}) collective-permute-start(bf16[8,64,512]{2,1,0:T(8,128)(2,1)} %get-tuple-element.14), channel_id=1, source_target_pairs={{0,2},{2,4},{4,6},{1,3},{3,5},{5,7},{8,10},{10,12},{12,14},{9,11},... | collective-permute-start | bytes 1572872 | tf_op jit(solution)/shard_map/ppermute | solution.py:188
  39.3 1.3 fusion
  40.6 2.1 %collective-permute-start.6 = (bf16[8,64,512]{2,1,0:T(8,128)(2,1)S(1)}, bf16[8,64,512]{2,1,0:T(8,128)(2,1)S(1)}, u32[]{:S(2)}, u32[]{:S(2)}) collective-permute-start(bf16[8,64,512]{2,1,0:T(8,128)(2,1)S(1)} %get-tuple-element.11), channel_id=1, source_target_pairs={{2,0},{4,2},{6,4},{3,1},{5,3},{7,5},{10,8},{12,10},{14,12},{11,9},... | collective-permute-start | bytes 1572872 | tf_op jit(solution)/shard_map/ppermute | solution.py:188
  42.8 3.8 %collective-permute-start.5 = (bf16[8,64,512]{2,1,0:T(8,128)(2,1)S(1)}, bf16[8,64,512]{2,1,0:T(8,128)(2,1)S(1)}, u32[]{:S(2)}, u32[]{:S(2)}) collective-permute-start(bf16[8,64,512]{2,1,0:T(8,128)(2,1)S(1)} %get-tuple-element.12), channel_id=1, source_target_pairs={{0,2},{2,4},{4,6},{1,3},{3,5},{5,7},{8,10},{10,12},{12,14},{9,11},... | collective-permute-start | bytes 1572872 | tf_op jit(solution)/shard_map/ppermute | solution.py:188
  46.6 0.9 constant_dynamic-slice_fusion.2
  47.5 2.0 %collective-permute-done.2.a_down = bf16[8,64,512]{2,1,0:T(8,128)(2,1)} collective-permute-done((bf16[8,64,512]{2,1,0:T(8,128)(2,1)}, bf16[8,64,512]{2,1,0:T(8,128)(2,1)}, u32[]{:S(2)}, u32[]{:S(2)}) %collective-permute-start.2) | collective-permute-done | bytes 524320 | tf_op jit(solution)/shard_map/ppermute | solution.py:188
  49.5 0.8 constant_dynamic-slice_fusion.4
  50.4 1.8 %collective-permute-done.1.a_up = bf16[8,64,512]{2,1,0:T(8,128)(2,1)S(1)} collective-permute-done((bf16[8,64,512]{2,1,0:T(8,128)(2,1)}, bf16[8,64,512]{2,1,0:T(8,128)(2,1)S(1)}, u32[]{:S(2)}, u32[]{:S(2)}) %collective-permute-start.1) | collective-permute-done | bytes 524320 | tf_op jit(solution)/shard_map/ppermute | solution.py:188
  52.2 0.3 collective-permute-start.3
  52.6 6.8 %collective-permute-done.6.m_down = bf16[8,64,512]{2,1,0:T(8,128)(2,1)S(1)} collective-permute-done((bf16[8,64,512]{2,1,0:T(8,128)(2,1)S(1)}, bf16[8,64,512]{2,1,0:T(8,128)(2,1)S(1)}, u32[]{:S(2)}, u32[]{:S(2)}) %collective-permute-start.6) | collective-permute-done | bytes 524320 | tf_op jit(solution)/shard_map/ppermute | solution.py:188
  59.3 2.7 %collective-permute-done.5.m_up = bf16[8,64,512]{2,1,0:T(8,128)(2,1)S(1)} collective-permute-done((bf16[8,64,512]{2,1,0:T(8,128)(2,1)S(1)}, bf16[8,64,512]{2,1,0:T(8,128)(2,1)S(1)}, u32[]{:S(2)}, u32[]{:S(2)}) %collective-permute-start.5) | collective-permute-done | bytes 524320 | tf_op jit(solution)/shard_map/ppermute | solution.py:188
  62.1 0.1 collective-permute-start.7
  62.2 8.2 %collective-permute-done.7.m_side = bf16[32,8,512]{2,1,0:T(8,128)(2,1)S(1)} collective-permute-done((bf16[32,8,512]{2,1,0:T(8,128)(2,1)S(1)}, bf16[32,8,512]{2,1,0:T(8,128)(2,1)S(1)}, u32[]{:S(2)}, u32[]{:S(2)}) %collective-permute-start.7) | collective-permute-done | bytes 262176 | tf_op jit(solution)/shard_map/ppermute | solution.py:199
  70.4 65.1 %transport.1 = (f32[16,64,512]{2,1,0:T(8,128)}, f32[16,64,512]{2,1,0:T(8,128)}) custom-call(f32[9,512]{1,0:T(8,128)S(1)} %get-tuple-element.18.wa_ref, f32[9,512]{1,0:T(8,128)S(1)} %get-tuple-element.17.wm_ref, bf16[16,64,512]{2,1,0:T(8,128)(2,1)S(1)} %collective-permute-done.a_mid, bf16[8,64,512]{2,1,0:T(8,128)(2,1)S(1)} %collective-permute-done.1.a_up, ...), custom_call_target="tpu_custom_call" | custom-call | flops 71303168 | bytes 18874368 | tf_op jit(solution)/shard_map/transport/pallas_call | solution.py:169
  (31 shorter events, 0.2 us)
Async XLA Ops:
  0.6 9.8 %copy-start = (s32[1,8]{1,0:T(1,128)S(1)}, s32[1,8]{1,0:T(1,128)}, u32[]{:S(2)}) copy-start(s32[1,8]{1,0:T(1,128)} %param.15) | copy-start | bytes 100
  0.6 6.7 %copy-start.2 = (f32[1,16,64,512]{3,2,1,0:T(8,128)S(1)}, f32[1,16,64,512]{3,2,1,0:T(8,128)}, u32[]{:S(2)}) copy-start(f32[1,16,64,512]{3,2,1,0:T(8,128)} %param.11) | copy-start | bytes 6291460
  3.5 7.5 %copy-start.1 = (f32[1,16,64,512]{3,2,1,0:T(8,128)S(1)}, f32[1,16,64,512]{3,2,1,0:T(8,128)}, u32[]{:S(2)}) copy-start(f32[1,16,64,512]{3,2,1,0:T(8,128)} %param.10) | copy-start | bytes 6291460
  3.5 7.5 %copy-start.10 = (s32[1,1,2048]{2,1,0:T(1,128)S(1)}, s32[1,1,2048]{2,1,0:T(1,128)}, u32[]{:S(2)}) copy-start(s32[1,1,2048]{2,1,0:T(1,128)} %param.14) | copy-start | bytes 24580
  3.5 7.5 %copy-start.11 = (f32[1024]{0:T(1024)S(1)}, f32[1024]{0:T(1024)}, u32[]{:S(2)}) copy-start(f32[1024]{0:T(1024)} %param.18) | copy-start | bytes 12292
  3.5 28.8 %collective-permute-start = (bf16[16,64,512]{2,1,0:T(8,128)(2,1)}, bf16[16,64,512]{2,1,0:T(8,128)(2,1)S(1)}, u32[]{:S(2)}, u32[]{:S(2)}) collective-permute-start(bf16[16,64,512]{2,1,0:T(8,128)(2,1)} %bitcast_convert_fusion.1), channel_id=1, source_target_pairs={{0,8},{8,16},{16,24},{1,9},{9,17},{17,25},{2,10},{10,18},{18,26},{... | collective-permute-start | bytes 3145736 | tf_op jit(solution)/shard_map/ppermute | solution.py:188
  8.5 30.9 %collective-permute-start.4 = (bf16[16,64,512]{2,1,0:T(8,128)(2,1)}, bf16[16,64,512]{2,1,0:T(8,128)(2,1)}, u32[]{:S(2)}, u32[]{:S(2)}) collective-permute-start(bf16[16,64,512]{2,1,0:T(8,128)(2,1)} %bitcast_convert_fusion), channel_id=1, source_target_pairs={{8,0},{16,8},{24,16},{9,1},{17,9},{25,17},{10,2},{18,10},{26,18},{... | collective-permute-start | bytes 3145736 | tf_op jit(solution)/shard_map/ppermute | solution.py:188
  11.0 1.6 %copy-start.6 = (bf16[1,1,2048,512]{3,2,1,0:T(8,128)(2,1)S(1)}, bf16[1,1,2048,512]{3,2,1,0:T(8,128)(2,1)}, u32[]{:S(2)}) copy-start(bf16[1,1,2048,512]{3,2,1,0:T(8,128)(2,1)} %param.13) | copy-start | bytes 6291460
  12.6 1.2 copy-start.7
  13.8 1.2 copy-start.8
  15.0 1.2 copy-start.9
  31.0 1.3 copy-start.4
  32.4 3.1 %copy-start.12 = (f32[8,512]{1,0:T(8,128)S(1)}, f32[8,512]{1,0:T(8,128)}, u32[]{:S(2)}) copy-start(f32[8,512]{1,0:T(8,128)} %param.16) | copy-start | bytes 49156
  33.4 16.1 %collective-permute-start.2 = (bf16[8,64,512]{2,1,0:T(8,128)(2,1)}, bf16[8,64,512]{2,1,0:T(8,128)(2,1)}, u32[]{:S(2)}, u32[]{:S(2)}) collective-permute-start(bf16[8,64,512]{2,1,0:T(8,128)(2,1)} %get-tuple-element.13), channel_id=1, source_target_pairs={{2,0},{4,2},{6,4},{3,1},{5,3},{7,5},{10,8},{12,10},{14,12},{11,9},... | collective-permute-start | bytes 1572872 | tf_op jit(solution)/shard_map/ppermute | solution.py:188
  35.8 34.6 %copy-start.3 = (f32[1,16,64,512]{3,2,1,0:T(8,128)S(1)}, f32[1,16,64,512]{3,2,1,0:T(8,128)}, u32[]{:S(2)}) copy-start(f32[1,16,64,512]{3,2,1,0:T(8,128)} %param.11) | copy-start | bytes 6291460
  35.9 34.6 %copy-start.5 = (f32[1024,512]{1,0:T(8,128)S(1)}, f32[1024,512]{1,0:T(8,128)}, u32[]{:S(2)}) copy-start(f32[1024,512]{1,0:T(8,128)} %copy-done.4) | copy-start | bytes 6291460
  35.9 16.3 %collective-permute-start.1 = (bf16[8,64,512]{2,1,0:T(8,128)(2,1)}, bf16[8,64,512]{2,1,0:T(8,128)(2,1)S(1)}, u32[]{:S(2)}, u32[]{:S(2)}) collective-permute-start(bf16[8,64,512]{2,1,0:T(8,128)(2,1)} %get-tuple-element.14), channel_id=1, source_target_pairs={{0,2},{2,4},{4,6},{1,3},{3,5},{5,7},{8,10},{10,12},{12,14},{9,11},... | collective-permute-start | bytes 1572872 | tf_op jit(solution)/shard_map/ppermute | solution.py:188
  40.6 18.7 %collective-permute-start.6 = (bf16[8,64,512]{2,1,0:T(8,128)(2,1)S(1)}, bf16[8,64,512]{2,1,0:T(8,128)(2,1)S(1)}, u32[]{:S(2)}, u32[]{:S(2)}) collective-permute-start(bf16[8,64,512]{2,1,0:T(8,128)(2,1)S(1)} %get-tuple-element.11), channel_id=1, source_target_pairs={{2,0},{4,2},{6,4},{3,1},{5,3},{7,5},{10,8},{12,10},{14,12},{11,9},... | collective-permute-start | bytes 1572872 | tf_op jit(solution)/shard_map/ppermute | solution.py:188
  42.8 19.3 %collective-permute-start.5 = (bf16[8,64,512]{2,1,0:T(8,128)(2,1)S(1)}, bf16[8,64,512]{2,1,0:T(8,128)(2,1)S(1)}, u32[]{:S(2)}, u32[]{:S(2)}) collective-permute-start(bf16[8,64,512]{2,1,0:T(8,128)(2,1)S(1)} %get-tuple-element.12), channel_id=1, source_target_pairs={{0,2},{2,4},{4,6},{1,3},{3,5},{5,7},{8,10},{10,12},{12,14},{9,11},... | collective-permute-start | bytes 1572872 | tf_op jit(solution)/shard_map/ppermute | solution.py:188
  52.2 10.0 %collective-permute-start.3 = (bf16[32,8,512]{2,1,0:T(8,128)(2,1)S(1)}, bf16[32,8,512]{2,1,0:T(8,128)(2,1)S(1)}, u32[]{:S(2)}, u32[]{:S(2)}) collective-permute-start(bf16[32,8,512]{2,1,0:T(8,128)(2,1)S(1)} %pad_maximum_fusion), channel_id=1, source_target_pairs={{0,1},{1,0},{2,3},{3,2},{4,5},{5,4},{6,7},{7,6},{8,9},{9,8},{10,11... | collective-permute-start | bytes 786440 | tf_op jit(solution)/shard_map/ppermute | solution.py:199
  62.1 8.3 %collective-permute-start.7 = (bf16[32,8,512]{2,1,0:T(8,128)(2,1)S(1)}, bf16[32,8,512]{2,1,0:T(8,128)(2,1)S(1)}, u32[]{:S(2)}, u32[]{:S(2)}) collective-permute-start(bf16[32,8,512]{2,1,0:T(8,128)(2,1)S(1)} %pad_maximum_fusion.1), channel_id=1, source_target_pairs={{0,1},{1,0},{2,3},{3,2},{4,5},{5,4},{6,7},{7,6},{8,9},{9,8},{10,11... | collective-permute-start | bytes 786440 | tf_op jit(solution)/shard_map/ppermute | solution.py:199

commit v2 on v1

v2 whole, which is shorter than its diff:
```python
import functools

import jax
import jax.numpy as jnp
from jax import lax
from jax.experimental import pallas as pl
from jax.experimental.pallas import tpu as pltpu
from jax.sharding import PartitionSpec as P

STEPS = 4
REACH = 2
HALO = STEPS * REACH
SUB = 8
LANES = 128
BLOCK = 4
MESH = pl.DeviceIdType.MESH
NT = (((1,), (1,)), ((), ()))
F32 = jnp.float32
BF16 = jnp.bfloat16


def dot(a, b):
    return jnp.dot(a, b, preferred_element_type=F32)


def dot_nt(a, b):
    return lax.dot_general(a, b, NT, preferred_element_type=F32)


CENTER, UP, DOWN, SIDE = 0, 2, 3, 4
KINDS = 7


def exchange_kernel(sizes, count_ref, cols_hbm, inc_hbm, mul_hbm, back_hbm, cot_hbm, hw_hbm, bias_hbm, ow_hbm,
                    field_out, side_out, tangent_out, adjoint_out,
                    cols, raw, sent, back, cot, hw, bias, ow, field, side, stage,
                    per_column, slot_cols, tangent, adjoint,
                    load_sem, send_sem, recv_sem, out_sem, tan_sem, adj_sem):
    n_sub, n_lat, n_lon = sizes
    sub, lat, lon = lax.axis_index("sub"), lax.axis_index("lat"), lax.axis_index("lon")
    height, across, levels = inc_hbm.shape
    columns = height * across
    slots = cot.shape[0]
    odd = sub % 2
    near, far = sub + 1 - 2 * odd, sub - 1 + 2 * odd
    has_near = near < n_sub
    has_far = jnp.logical_and(far >= 0, far < n_sub)
    near_field, far_field = 1 - odd, odd
    has_above, has_below = lat > 0, lat < n_lat - 1

    loads = [(inc_hbm, raw.at[0]), (mul_hbm, raw.at[1]), (cols_hbm, cols), (cot_hbm, cot), (back_hbm, back),
             (hw_hbm, hw), (bias_hbm, bias), (ow_hbm, ow)]
    loads = [pltpu.make_async_copy(a, b, load_sem.at[k]) for k, (a, b) in enumerate(loads)]
    for load in loads:
        load.start()

    barrier = pltpu.get_barrier_semaphore()
    others = [({"sub": near}, has_near), ({"sub": far}, has_far), ({"lat": lat - 1}, has_above), ({"lat": lat + 1}, has_below)]
    amount = sum(have.astype(jnp.int32) for _, have in others)
    for target, have in others:
        @pl.when(have)
        def _(target=target):
            pl.semaphore_signal(barrier, inc=1, device_id=target, device_id_type=MESH)
    if n_lon > 1:
        pl.semaphore_signal(barrier, inc=1, device_id={"lon": 1 - lon}, device_id_type=MESH)
        amount = amount + 1

    def copy(f, kind, src, dst, target):
        return pltpu.make_async_remote_copy(src_ref=src, dst_ref=dst, send_sem=send_sem.at[f, kind],
                                            recv_sem=recv_sem.at[f, kind], device_id=target, device_id_type=MESH)

    def center(f, part, target):
        return copy(f, CENTER + part, sent.at[f, pl.ds(part * HALO, HALO)],
                    field.at[f, pl.ds(HALO + part * HALO, HALO)], target)

    def upward(f):
        return copy(f, DOWN, field.at[f, pl.ds(HALO, HALO)], field.at[f, pl.ds(HALO + height, HALO)], {"lat": lat - 1})

    def downward(f):
        return copy(f, UP, field.at[f, pl.ds(height, HALO)], field.at[f, pl.ds(0, HALO)], {"lat": lat + 1})

    def sideways(f, k):
        lo, amount = ((HALO // 2, height // 2), (0, HALO // 2), ((HALO + height) // 2, HALO // 2))[k]
        return copy(f, SIDE + k, stage.at[f, pl.ds(lo, amount)], side.at[f, pl.ds(lo, amount)], {"lon": 1 - lon})

    def keep(f, k):
        lo, amount = ((HALO, height), (0, HALO), (HALO + height, HALO))[k]
        rows = pl.ds(lo, amount)
        return pltpu.make_async_copy(field.at[f, rows], field_out.at[f, rows], out_sem.at[f, k])

    def pass_on(f, k):
        keep(f, k).start()
        if n_lon > 1:
            lo, amount = ((HALO // 2, height // 2), (0, HALO // 2), ((HALO + height) // 2, HALO // 2))[k]

            @pl.loop(lo, lo + amount)
            def _(p):
                pair = []
                for q in range(2):
                    row = field[f, 2 * p + q].astype(F32)
                    pair.append(jnp.where(lon == 0, row[across - HALO:], row[:HALO]))
                stage[f, p] = jnp.concatenate(pair, axis=0).astype(BF16)
            sideways(f, k).start()

    def take_center(f, source):
        center(f, 0, {"sub": source}).wait_recv()

        @pl.when(has_above)
        def _():
            upward(f).start()
        center(f, 1, {"sub": source}).wait_recv()

        @pl.when(has_below)
        def _():
            downward(f).start()
        pass_on(f, 0)

    def take_halo(f):
        @pl.when(has_above)
        def _():
            downward(f).wait_recv()
            pass_on(f, 1)

        @pl.when(has_below)
        def _():
            upward(f).wait_recv()
            pass_on(f, 2)

    def finish(f):
        def close(k):
            keep(f, k).wait()
            if n_lon > 1:
                sideways(f, k).wait()
        close(0)

        @pl.when(has_above)
        def _():
            upward(f).wait_send()
            close(1)

        @pl.when(has_below)
        def _():
            downward(f).wait_send()
            close(2)

    loads[0].wait()
    sent[0] = raw[0].astype(BF16)
    loads[1].wait()
    sent[1] = raw[1].astype(BF16)
    pl.semaphore_wait(barrier, amount)

    @pl.when(has_far)
    def _():
        for part in range(2):
            center(near_field, part, {"sub": far}).start()

    @pl.when(has_near)
    def _():
        for part in range(2):
            center(far_field, part, {"sub": near}).start()

    for load in loads[2:]:
        load.wait()
    count = count_ref[0]
    tile = 256
    chunks = slots // LANES
    place = (lax.broadcasted_iota(jnp.int32, (chunks, LANES), 0) * LANES
             + lax.broadcasted_iota(jnp.int32, (chunks, LANES), 1))
    slot_cols[...] = jnp.where(place < count, cols[...], -1)

    def adjoint_copy(t):
        rows = pl.ds(pl.multiple_of(t * tile, tile), tile)
        return pltpu.make_async_copy(adjoint.at[rows], adjoint_out.at[rows], adj_sem.at[t])

    def tangent_copy(t):
        rows = pl.ds(pl.multiple_of(t * tile, tile), tile)
        return pltpu.make_async_copy(tangent.at[rows], tangent_out.at[rows], tan_sem.at[t])

    def observe_columns(t):
        base = pl.multiple_of(t * tile, tile)
        rows = pl.ds(base, tile)
        wanted = lax.broadcasted_iota(jnp.int32, (tile, LANES), 0) + base
        hits = [jnp.where(slot_cols[k:k + 1, :] == wanted, 1.0, 0.0).astype(BF16) for k in range(chunks)]
        summed = dot(jnp.concatenate(hits, axis=1), cot[...]).astype(BF16)
        hidden = jnp.tanh(dot(back[rows, :], hw[...]) + bias[...])
        slopes = 1.0 - hidden * hidden
        state = sent[0, pl.ds(t * (tile // across), tile // across)].reshape(tile, levels)
        forward = dot(state, hw[...])
        per_column[rows, :] = dot((slopes * forward).astype(BF16), ow[...]).astype(BF16)
        pulled = dot_nt(summed, ow[...])
        adjoint[rows, :] = dot_nt((slopes * pulled).astype(BF16), hw[...])
        adjoint_copy(t).start()

    def observe_slots(t):
        parts = []
        for h in range(tile // LANES):
            named = jnp.transpose(jnp.broadcast_to(slot_cols[pl.ds(t * (tile // LANES) + h, 1), :], (LANES, LANES)))
            lane = lax.broadcasted_iota(jnp.int32, (LANES, LANES), 1)
            hits = [jnp.where(named == lane + c * LANES, 1.0, 0.0).astype(BF16) for c in range(columns // LANES)]
            parts.append(jnp.concatenate(hits, axis=1))
        tangent[pl.ds(pl.multiple_of(t * tile, tile), tile), :] = dot(
            jnp.concatenate(parts, axis=0), per_column[...]).astype(BF16)
        tangent_copy(t).start()

    column_tiles, slot_tiles = columns // tile, slots // tile
    pl.loop(0, 1)(observe_columns)

    @pl.when(has_near)
    def _():
        take_center(near_field, near)
    pl.loop(1, column_tiles)(observe_columns)

    @pl.when(has_far)
    def _():
        take_center(far_field, far)
    pl.loop(0, slot_tiles // 2)(observe_slots)

    @pl.when(has_near)
    def _():
        take_halo(near_field)
    pl.loop(slot_tiles // 2, slot_tiles)(observe_slots)

    @pl.when(has_far)
    def _():
        take_halo(far_field)

    for have, f, source in ((has_near, near_field, near), (has_far, far_field, far)):
        @pl.when(have)
        def _(f=f, source=source):
            finish(f)
            for part in range(2):
                center(1 - f, part, {"sub": source}).wait_send()

    if n_lon > 1:
        kept = pltpu.make_async_copy(side, side_out, load_sem.at[0])
        kept.start()
        kept.wait()
    for t in range(column_tiles):
        adjoint_copy(t).wait()
    for t in range(slot_tiles):
        tangent_copy(t).wait()


def exchange(sizes, count, cols, inc, mul, back, cot, hw, bias, ow):
    height, across, levels = inc.shape
    columns = height * across
    slots, chan = cot.shape
    hid = hw.shape[1]
    total = height + 2 * HALO
    anywhere = pl.BlockSpec(memory_space=pl.ANY)
    vm = pltpu.VMEM
    dma = pltpu.SemaphoreType.DMA
    field_shape, side_shape = (2, total, across, levels), (2, total // 2, 2 * HALO, levels)
    flops = 2 * columns * levels * hid * 5 + 4 * columns * slots * chan
    return pl.pallas_call(
        functools.partial(exchange_kernel, sizes),
        out_shape=(jax.ShapeDtypeStruct(field_shape, BF16), jax.ShapeDtypeStruct(side_shape, BF16),
                   jax.ShapeDtypeStruct((slots, chan), BF16), jax.ShapeDtypeStruct((columns, levels), F32)),
        in_specs=[pl.BlockSpec(memory_space=pltpu.SMEM)] + [anywhere] * 8,
        out_specs=(anywhere,) * 4,
        scratch_shapes=[
            vm(cols.shape, jnp.int32), vm((2,) + inc.shape, F32), vm((2,) + inc.shape, BF16),
            vm(back.shape, BF16), vm(cot.shape, BF16), vm(hw.shape, BF16), vm(bias.shape, F32), vm(ow.shape, BF16),
            vm(field_shape, BF16), vm(side_shape, BF16), vm(side_shape, BF16),
            vm((columns, chan), BF16), vm(cols.shape, jnp.int32), vm((slots, chan), BF16), vm((columns, levels), F32),
            dma((8,)), dma((2, KINDS)), dma((2, KINDS)), dma((2, 3)), dma((slots // 256,)), dma((columns // 256,)),
        ],
        compiler_params=pltpu.CompilerParams(vmem_limit_bytes=52 << 20, collective_id=0, has_side_effects=True),
        cost_estimate=pl.CostEstimate(flops=flops, bytes_accessed=20 << 20, transcendentals=columns * hid),
        name="exchange",
    )(count, cols, inc, mul, back, cot, hw, bias, ow)


def transport_field(lat_first, lat_last, start, side_at, field, side, f, weights, window, one, two, width, n_lon):
    total, across = field.shape[1], field.shape[2]
    window[:, pl.ds(start, across), :] = field[f].astype(F32)
    if n_lon > 1:
        for p in range(total // 2):
            pair = side[f, p].astype(F32)
            window[2 * p, pl.ds(side_at, HALO), :] = pair[:HALO]
            window[2 * p + 1, pl.ds(side_at, HALO), :] = pair[HALO:]

    lane_row = lax.broadcasted_iota(jnp.int32, (SUB, LANES), 0)
    low_edge = lane_row == 0
    high_edge = lane_row == SUB - 1

    def put(ref, r, v, vec):
        ref[r, v + REACH] = vec
        if v >= width - REACH:
            ref[r, v - (width - REACH)] = jnp.where(low_edge, 0.0, pltpu.roll(vec, 1, 0))
        if v < REACH:
            ref[r, v + width + REACH] = jnp.where(high_edge, 0.0, pltpu.roll(vec, SUB - 1, 0))

    def clear_outside(ref):
        zero = jnp.zeros((HALO,) + ref.shape[1:], F32)

        @pl.when(lat_first)
        def _():
            ref[pl.ds(0, HALO)] = zero

        @pl.when(lat_last)
        def _():
            ref[pl.ds(total - HALO, HALO)] = zero

    @pl.loop(0, total // 2)
    def _(p):
        for q in range(2):
            for v in range(width):
                put(one, 2 * p + q, v, window[2 * p + q, pl.ds(v, SUB, stride=width), :])
    clear_outside(one)

    c = [jnp.broadcast_to(weights[k:k + 1, :], (SUB, LANES)) for k in range(9)]
    for step in range(STEPS):
        src, dst = (one, two) if step % 2 == 0 else (two, one)
        lo = REACH * (step + 1)

        @pl.loop(0, (total - 2 * lo) // BLOCK)
        def _(b):
            r = lo + b * BLOCK
            for v in range(width):
                tall = [src[r + k - REACH, v + REACH] for k in range(BLOCK + 2 * REACH)]
                for q in range(BLOCK):
                    line = [src[r + q, v + k] for k in (0, 1, 3, 4)]
                    acc = ((c[8] * tall[q + 2] + c[0] * tall[q]) + (c[1] * tall[q + 1] + c[2] * tall[q + 3])
                           + (c[3] * tall[q + 4] + c[5] * line[1])
                           + ((c[4] * line[0] + c[6] * line[2]) + c[7] * line[3]))
                    if step == STEPS - 1:
                        window[r + q, pl.ds(v, SUB, stride=width), :] = acc
                    else:
                        put(dst, r + q, v, acc)
        if step < STEPS - 1:
            clear_outside(dst)


def transport_kernel(sizes, width, wa_ref, wm_ref, field, side, inc_ref, mul_ref, adj_ref, err_ref, grad_ref,
                     window, one, two):
    n_sub, n_lat, n_lon = sizes
    sub, lat, lon = lax.axis_index("sub"), lax.axis_index("lat"), lax.axis_index("lon")
    height, across = inc_ref.shape[0], inc_ref.shape[1]
    start = pl.multiple_of(jnp.where(lon == 0, 0, HALO), HALO) if n_lon > 1 else 0
    side_at = pl.multiple_of(jnp.where(lon == 0, across, 0), HALO)
    place = (lat == 0, lat == n_lat - 1, start, side_at, field, side)
    rest = (window, one, two, width, n_lon)
    result = (pl.ds(HALO, height), pl.ds(start, across))

    @pl.when(sub > 0)
    def _():
        transport_field(*place, 0, wa_ref, *rest)
        err_ref[...] = inc_ref[...] - window[result]

    @pl.when(sub == 0)
    def _():
        err_ref[...] = inc_ref[...]

    @pl.when(sub < n_sub - 1)
    def _():
        transport_field(*place, 1, wm_ref, *rest)
        grad_ref[...] = mul_ref[...] - window[result] + adj_ref[...]

    @pl.when(sub == n_sub - 1)
    def _():
        grad_ref[...] = mul_ref[...] + adj_ref[...]


def transport_call(sizes, wa, wm, field, side, inc, mul, adj):
    height, across, levels = inc.shape
    width = (across + (HALO if sizes[2] > 1 else 0)) // SUB
    total = height + 2 * HALO
    def whole(shape):
        return pl.BlockSpec(shape[:-1] + (LANES,), lambda g: (0,) * (len(shape) - 1) + (g,))
    arrays = (wa, wm, field, side, inc, mul, adj)
    state = pltpu.VMEM((total, width + 2 * REACH, SUB, LANES), F32)
    return pl.pallas_call(
        functools.partial(transport_kernel, sizes, width),
        grid=(levels // LANES,),
        out_shape=(jax.ShapeDtypeStruct(inc.shape, F32),) * 2,
        in_specs=[whole(x.shape) for x in arrays],
        out_specs=(whole(inc.shape),) * 2,
        scratch_shapes=[pltpu.VMEM((total, width * SUB, LANES), F32), state, state],
        compiler_params=pltpu.CompilerParams(vmem_limit_bytes=40 << 20),
        cost_estimate=pl.CostEstimate(flops=2 * 4 * 17 * height * across * levels, bytes_accessed=18 << 20, transcendentals=0),
        name="transport",
    )(*arrays)


def local(increment, multiplier, background, obs_cotangent, obs_column, obs_count, transport,
          hidden_weight, hidden_bias, output_weight):
    sizes = tuple(lax.axis_size(name) for name in ("sub", "lat", "lon"))
    assert sizes[2] <= 2
    inc, mul = increment[0], multiplier[0]
    levels = inc.shape[-1]
    rest = (1.0 - jnp.sum(transport, axis=0))[None]
    wa = jnp.concatenate([transport, rest], axis=0)
    wm = jnp.concatenate([transport[3::-1], transport[7:3:-1], rest], axis=0)
    myself = lax.axis_index(("lat", "lon"))
    count = lax.dynamic_slice_in_dim(obs_count[0], myself, 1)
    field, side, tangent, adj = exchange(
        sizes, count, obs_column.reshape(-1, LANES), inc, mul, background.reshape(-1, levels), obs_cotangent[0, 0],
        hidden_weight, hidden_bias[None], output_weight)
    err, grad = transport_call(sizes, wa, wm, field, side, inc, mul, adj.reshape(inc.shape))
    return err[None], grad[None], tangent[None, None]


def solution(mesh):
    field = P("sub", "lat", "lon", None)
    slots = P("sub", ("lat", "lon"), None, None)
    in_specs = (field, field, field, slots, P("sub", ("lat", "lon"), None), P("sub", None), P(), P(), P(), P())
    return jax.shard_map(local, mesh=mesh, in_specs=in_specs, out_specs=(field, field, slots), check_vma=False)
```

time: 136 us -> 65.3 us (0.48)
  the two profiles are of different devices: /device:TPU:13 before, /device:TPU:1 now
where the time goes in v2:
time: 65.3 us; the launch traced here: 64.6 us
  Pallas kernels  52.4 us (80%)
  local copies, waits for them, and re-layouts  9.96 us (15%)
  other arithmetic  1.47 us (2%)
  between operations  0.71 us (1%)
    pallas_call x1, Pallas kernels, exchange(): pl.pallas_call(functools.partial(exchange_kernel, sizes), out_shape=(jax....  30.1 us
    pallas_call x1, Pallas kernels, transport_call(): pl.pallas_call(functools.partial(transport_kernel, sizes, width), grid=(l...  22.3 us
    unnamed x19, local copies, waits for them, and re-layouts  8.35 us

profile of v2, /device:TPU:1, one launch (start us, length us, event | category | flops | bytes accessed | tf_op | source)
XLA Modules:
  0.0 64.6 jit_solution(341966643059326437)
XLA Ops:
  0.6 0.0 copy-start
  0.7 0.6 copy-done
  1.3 0.6 constant_dynamic-slice_fusion
  1.9 0.7 %reduce_sum.9 = f32[512]{0:T(512)S(1)} reduce(f32[8,512]{1,0:T(8,128)} %param.16, f32[]{:T(128)} %constant.4.clone.1), dimensions={0}, to_apply=%region_0.0 | reduce | flops 3584 | bytes 18436 | tf_op jit(solution)/shard_map/reduce_sum | solution.py:392
  2.6 0.8 %fusion = (f32[4,512]{1,0:T(4,128)S(1)}, f32[4,512]{1,0:T(4,128)S(1)}) fusion(f32[8,512]{1,0:T(8,128)} %param.16), kind=kLoop, calls=%fused_computation.4 | loop fusion | bytes 32768 | tf_op jit(solution)/shard_map/slice | solution.py:394
  3.4 0.1 rev.6
  3.5 0.1 rev.7
  3.7 0.7 %pad_maximum_fusion = (f32[9,512]{1,0:T(8,128)S(1)}, f32[9,512]{1,0:T(8,128)S(1)}) fusion(f32[1,512]{1,0:T(1,128)S(1)} %bitcast.21, f32[4,512]{1,0:T(4,128)S(1)} %rev.7, f32[4,512]{1,0:T(4,128)S(1)} %rev.6, f32[8,512]{1,0:T(8,128)} %param.16), kind=kLoop, calls=%fused_computation | loop fusion | flops 13824 | bytes 71680 | tf_op jit(solution)/shard_map/concatenate | solution.py:394
  4.4 0.0 copy-start.5
  4.4 1.2 %copy-done.5 = bf16[1,16,64,512]{3,2,1,0:T(8,128)(2,1)S(1)} copy-done((bf16[1,16,64,512]{3,2,1,0:T(8,128)(2,1)S(1)}, bf16[1,16,64,512]{3,2,1,0:T(8,128)(2,1)}, u32[]{:S(2)}) %copy-start.5) | copy-done | bytes 1048600
  5.6 0.0 copy-start.6
  5.6 0.7 %copy-done.6 = s32[1,1,2048]{2,1,0:T(1,128)S(1)} copy-done((s32[1,1,2048]{2,1,0:T(1,128)S(1)}, s32[1,1,2048]{2,1,0:T(1,128)}, u32[]{:S(2)}) %copy-start.6) | copy-done | bytes 8216
  6.3 0.0 copy-start.7
  6.3 0.7 %copy-done.7 = f32[1024]{0:T(1024)S(1)} copy-done((f32[1024]{0:T(1024)S(1)}, f32[1024]{0:T(1024)}, u32[]{:S(2)}) %copy-start.7) | copy-done | bytes 4120
  7.0 0.0 copy-start.2
  7.0 0.0 copy-start.3
  7.0 30.1 %exchange.1 = (bf16[2,32,64,512]{3,2,1,0:T(8,128)(2,1)}, bf16[2,16,16,512]{3,2,1,0:T(8,128)(2,1)S(1)}, bf16[2048,512]{1,0:T(8,128)(2,1)}, f32[1024,512]{1,0:T(8,128)}) custom-call(s32[1]{0:T(128)} %bitcast.1.count_ref, s32[16,128]{1,0:T(8,128)S(1)} %bitcast.18, f32[16,64,512]{2,1,0:T(8,128)} %bitcast.12, f32[16,64,512]{2,1,0:T(8,128)} %bitcast.14, ...), custom_call_target="tpu_custom_call" | custom-call | flops 9663676416 | bytes 20971520 | tf_op jit(solution)/shard_map/exchange/pallas_call | solution.py:255
  37.1 0.0 copy-done.2
  37.1 0.0 copy-done.3
  37.1 0.0 copy-start.1
  37.1 2.2 %copy-done.1 = bf16[2,32,64,512]{3,2,1,0:T(8,128)(2,1)S(1)} copy-done((bf16[2,32,64,512]{3,2,1,0:T(8,128)(2,1)S(1)}, bf16[2,32,64,512]{3,2,1,0:T(8,128)(2,1)}, u32[]{:S(2)}) %copy-start.1) | copy-done | bytes 4194328
  39.3 0.0 copy-start.4
  39.3 1.6 %copy-done.4 = f32[1024,512]{1,0:T(8,128)S(1)} copy-done((f32[1024,512]{1,0:T(8,128)S(1)}, f32[1024,512]{1,0:T(8,128)}, u32[]{:S(2)}) %copy-start.4) | copy-done | bytes 2097176
  40.9 0.0 copy-start.8
  40.9 22.3 %transport.1 = (f32[16,64,512]{2,1,0:T(8,128)}, f32[16,64,512]{2,1,0:T(8,128)}) custom-call(f32[9,512]{1,0:T(8,128)S(1)} %get-tuple-element.18.wa_ref, f32[9,512]{1,0:T(8,128)S(1)} %get-tuple-element.17.wm_ref, bf16[2,32,64,512]{3,2,1,0:T(8,128)(2,1)S(1)} %copy-done.1, bf16[2,16,16,512]{3,2,1,0:T(8,128)(2,1)S(1)} %get-tuple-element.10.side, ...), custom_call_target="tpu_custom_call" | custom-call | flops 71303168 | bytes 18874368 | tf_op jit(solution)/shard_map/transport/pallas_call | solution.py:373
  63.3 0.0 copy-done.8
  63.3 1.3 %copy.14 = bf16[1,1,2048,512]{3,2,1,0:T(8,128)(2,1)} copy(bf16[1,1,2048,512]{3,2,1,0:T(8,128)(2,1)S(1)} %bitcast.20) | data formatting | bytes 4194304
  (1 shorter events, 0.0 us)
Async XLA Ops:
  0.6 0.7 %copy-start = (s32[1,8]{1,0:T(1,128)S(1)}, s32[1,8]{1,0:T(1,128)}, u32[]{:S(2)}) copy-start(s32[1,8]{1,0:T(1,128)} %param.15) | copy-start | bytes 100
  4.4 1.2 %copy-start.5 = (bf16[1,16,64,512]{3,2,1,0:T(8,128)(2,1)S(1)}, bf16[1,16,64,512]{3,2,1,0:T(8,128)(2,1)}, u32[]{:S(2)}) copy-start(bf16[1,16,64,512]{3,2,1,0:T(8,128)(2,1)} %param.12) | copy-start | bytes 3145732
  5.6 0.7 %copy-start.6 = (s32[1,1,2048]{2,1,0:T(1,128)S(1)}, s32[1,1,2048]{2,1,0:T(1,128)}, u32[]{:S(2)}) copy-start(s32[1,1,2048]{2,1,0:T(1,128)} %param.14) | copy-start | bytes 24580
  6.3 0.7 %copy-start.7 = (f32[1024]{0:T(1024)S(1)}, f32[1024]{0:T(1024)}, u32[]{:S(2)}) copy-start(f32[1024]{0:T(1024)} %param.18) | copy-start | bytes 12292
  7.0 30.1 %copy-start.2 = (f32[1,16,64,512]{3,2,1,0:T(8,128)S(1)}, f32[1,16,64,512]{3,2,1,0:T(8,128)}, u32[]{:S(2)}) copy-start(f32[1,16,64,512]{3,2,1,0:T(8,128)} %param.10) | copy-start | bytes 6291460
  7.0 30.1 %copy-start.3 = (f32[1,16,64,512]{3,2,1,0:T(8,128)S(1)}, f32[1,16,64,512]{3,2,1,0:T(8,128)}, u32[]{:S(2)}) copy-start(f32[1,16,64,512]{3,2,1,0:T(8,128)} %param.11) | copy-start | bytes 6291460
  37.1 2.2 %copy-start.1 = (bf16[2,32,64,512]{3,2,1,0:T(8,128)(2,1)S(1)}, bf16[2,32,64,512]{3,2,1,0:T(8,128)(2,1)}, u32[]{:S(2)}) copy-start(bf16[2,32,64,512]{3,2,1,0:T(8,128)(2,1)} %get-tuple-element.9.field) | copy-start | bytes 12582916
  39.3 1.6 %copy-start.4 = (f32[1024,512]{1,0:T(8,128)S(1)}, f32[1024,512]{1,0:T(8,128)}, u32[]{:S(2)}) copy-start(f32[1024,512]{1,0:T(8,128)} %get-tuple-element.11) | copy-start | bytes 6291460
  40.9 22.3 %copy-start.8 = (bf16[2048,512]{1,0:T(8,128)(2,1)S(1)}, bf16[2048,512]{1,0:T(8,128)(2,1)}, u32[]{:S(2)}) copy-start(bf16[2048,512]{1,0:T(8,128)(2,1)} %get-tuple-element.14) | copy-start | bytes 6291460

commit v3 on v2

v3 whole, which is shorter than its diff:
```python
import functools

import jax
import jax.numpy as jnp
from jax import lax
from jax.experimental import pallas as pl
from jax.experimental.pallas import tpu as pltpu
from jax.sharding import PartitionSpec as P

STEPS = 4
REACH = 2
HALO = STEPS * REACH
SUB = 8
LANES = 128
BLOCK = 4
MESH = pl.DeviceIdType.MESH
NT = (((1,), (1,)), ((), ()))
F32 = jnp.float32
BF16 = jnp.bfloat16


def dot(a, b):
    return jnp.dot(a, b, preferred_element_type=F32)


def dot_nt(a, b):
    return lax.dot_general(a, b, NT, preferred_element_type=F32)


CENTER, UP, DOWN, SIDE = 0, 2, 3, 4
DIRECT = 7
KINDS = 9
VMEM_BYTES = 58 << 20


def exchange_kernel(sizes, count_ref, cols_hbm, inc_hbm, mul_hbm, back_hbm, cot_hbm, hw_hbm, bias_hbm, ow_hbm, rates_hbm,
                    field_out, side_out, tangent_out, adjoint_out, moved_out,
                    rates, moved, window, one, two, cols, raw, sent, back, cot, hw, bias, ow, field, side, stage,
                    per_column, slot_cols, tangent, adjoint,
                    load_sem, send_sem, recv_sem, out_sem, tan_sem, adj_sem, moved_sem):
    n_sub, n_lat, n_lon = sizes
    sub, lat, lon = lax.axis_index("sub"), lax.axis_index("lat"), lax.axis_index("lon")
    height, across, levels = inc_hbm.shape
    columns = height * across
    slots = cot.shape[0]
    odd = sub % 2
    near, far = sub + 1 - 2 * odd, sub - 1 + 2 * odd
    has_near = near < n_sub
    has_far = jnp.logical_and(far >= 0, far < n_sub)
    near_field, far_field = 1 - odd, odd
    has_above, has_below = lat > 0, lat < n_lat - 1

    loads = [(inc_hbm, raw.at[0]), (mul_hbm, raw.at[1]), (cols_hbm, cols), (cot_hbm, cot), (back_hbm, back),
             (hw_hbm, hw), (bias_hbm, bias), (ow_hbm, ow), (rates_hbm, rates)]
    loads = [pltpu.make_async_copy(a, b, load_sem.at[k]) for k, (a, b) in enumerate(loads)]
    for load in loads[:2]:
        load.start()

    barrier = pltpu.get_barrier_semaphore()
    near_above, near_below = jnp.logical_and(has_near, has_above), jnp.logical_and(has_near, has_below)
    others = [({"sub": near}, has_near), ({"sub": far}, has_far), ({"lat": lat - 1}, has_above), ({"lat": lat + 1}, has_below),
              ({"sub": near, "lat": lat - 1}, near_above), ({"sub": near, "lat": lat + 1}, near_below)]
    amount = sum(have.astype(jnp.int32) for _, have in others)
    for target, have in others:
        @pl.when(have)
        def _(target=target):
            pl.semaphore_signal(barrier, inc=1, device_id=target, device_id_type=MESH)
    if n_lon > 1:
        pl.semaphore_signal(barrier, inc=1, device_id={"lon": 1 - lon}, device_id_type=MESH)
        amount = amount + 1

    def copy(f, kind, src, dst, target):
        return pltpu.make_async_remote_copy(src_ref=src, dst_ref=dst, send_sem=send_sem.at[f, kind],
                                            recv_sem=recv_sem.at[f, kind], device_id=target, device_id_type=MESH)

    def center(f, part, target):
        return copy(f, CENTER + part, sent.at[f, pl.ds(part * HALO, HALO)],
                    field.at[f, pl.ds(HALO + part * HALO, HALO)], target)

    def upward(f):
        return copy(f, DOWN, field.at[f, pl.ds(HALO, HALO)], field.at[f, pl.ds(HALO + height, HALO)], {"lat": lat - 1})

    def downward(f):
        return copy(f, UP, field.at[f, pl.ds(height, HALO)], field.at[f, pl.ds(0, HALO)], {"lat": lat + 1})

    def direct(k):
        f, src, dst, row = ((far_field, 0, HALO + height, lat - 1), (far_field, height - HALO, 0, lat + 1))[k]
        return pltpu.make_async_remote_copy(
            src_ref=sent.at[f, pl.ds(src, HALO)], dst_ref=field.at[f, pl.ds(dst, HALO)],
            send_sem=send_sem.at[f, DIRECT + k], recv_sem=recv_sem.at[f, (DOWN, UP)[k]],
            device_id={"sub": near, "lat": row}, device_id_type=MESH)

    def sideways(f, k):
        lo, amount = ((HALO // 2, height // 2), (0, HALO // 2), ((HALO + height) // 2, HALO // 2))[k]
        return copy(f, SIDE + k, stage.at[f, pl.ds(lo, amount)], side.at[f, pl.ds(lo, amount)], {"lon": 1 - lon})

    def keep(f, k):
        lo, amount = ((HALO, height), (0, HALO), (HALO + height, HALO))[k]
        rows = pl.ds(lo, amount)
        return pltpu.make_async_copy(field.at[f, rows], field_out.at[rows], out_sem.at[k])

    def pass_on(f, k, stored=False):
        if stored:
            keep(f, k).start()
        if n_lon > 1:
            lo, amount = ((HALO // 2, height // 2), (0, HALO // 2), ((HALO + height) // 2, HALO // 2))[k]

            @pl.loop(lo, lo + amount)
            def _(p):
                pair = []
                for q in range(2):
                    row = field[f, 2 * p + q].astype(F32)
                    pair.append(jnp.where(lon == 0, row[across - HALO:], row[:HALO]))
                stage[f, p] = jnp.concatenate(pair, axis=0).astype(BF16)
            sideways(f, k).start()

    def take_near_center():
        center(near_field, 0, {"sub": near}).wait_recv()
        center(near_field, 1, {"sub": near}).wait_recv()
        pass_on(near_field, 0)

    def take_far_center():
        center(far_field, 0, {"sub": far}).wait_recv()

        @pl.when(has_above)
        def _():
            upward(far_field).start()
        center(far_field, 1, {"sub": far}).wait_recv()

        @pl.when(has_below)
        def _():
            downward(far_field).start()
        pass_on(far_field, 0, True)

    def take_halo(f, stored=False):
        @pl.when(has_above)
        def _():
            downward(f).wait_recv()
            pass_on(f, 1, stored)

        @pl.when(has_below)
        def _():
            upward(f).wait_recv()
            pass_on(f, 2, stored)

    def settle(f):
        if n_lon > 1:
            sideways(f, 0).wait()

            @pl.when(has_above)
            def _():
                sideways(f, 1).wait()

            @pl.when(has_below)
            def _():
                sideways(f, 2).wait()

    def cast(f):
        pltpu.make_async_copy(inc_hbm, raw.at[f], load_sem.at[f]).wait()
        for part in range(2):
            rows = pl.ds(part * HALO, HALO)
            sent[f, rows] = raw[f, rows].astype(BF16)

    cast(near_field)
    pl.semaphore_wait(barrier, amount)

    @pl.when(has_far)
    def _():
        for part in range(2):
            center(near_field, part, {"sub": far}).start()
    cast(far_field)

    @pl.when(near_above)
    def _():
        direct(0).start()

    @pl.when(near_below)
    def _():
        direct(1).start()

    @pl.when(has_near)
    def _():
        for part in range(2):
            center(far_field, part, {"sub": near}).start()

    for load in loads[2:]:
        load.start()
    for load in loads[2:]:
        load.wait()
    count = count_ref[lat * n_lon + lon]
    tile = 256
    chunks = slots // LANES
    place = (lax.broadcasted_iota(jnp.int32, (chunks, LANES), 0) * LANES
             + lax.broadcasted_iota(jnp.int32, (chunks, LANES), 1))
    slot_cols[...] = jnp.where(place < count, cols[...], -1)

    def adjoint_copy(t):
        rows = pl.ds(pl.multiple_of(t * tile, tile), tile)
        return pltpu.make_async_copy(adjoint.at[rows], adjoint_out.at[rows], adj_sem.at[t])

    def tangent_copy(t):
        rows = pl.ds(pl.multiple_of(t * tile, tile), tile)
        return pltpu.make_async_copy(tangent.at[rows], tangent_out.at[rows], tan_sem.at[t])

    def observe_columns(t):
        base = pl.multiple_of(t * tile, tile)
        rows = pl.ds(base, tile)
        wanted = lax.broadcasted_iota(jnp.int32, (tile, LANES), 0) + base
        hits = [jnp.where(slot_cols[k:k + 1, :] == wanted, 1.0, 0.0).astype(BF16) for k in range(chunks)]
        summed = dot(jnp.concatenate(hits, axis=1), cot[...]).astype(BF16)
        hidden = jnp.tanh(dot(back[rows, :], hw[...]) + bias[...])
        slopes = 1.0 - hidden * hidden
        state = sent[0, pl.ds(t * (tile // across), tile // across)].reshape(tile, levels)
        forward = dot(state, hw[...])
        per_column[rows, :] = dot((slopes * forward).astype(BF16), ow[...]).astype(BF16)
        pulled = dot_nt(summed, ow[...])
        adjoint[rows, :] = dot_nt((slopes * pulled).astype(BF16), hw[...])
        adjoint_copy(t).start()

    def observe_slots(t):
        parts = []
        for h in range(tile // LANES):
            named = jnp.transpose(jnp.broadcast_to(slot_cols[pl.ds(t * (tile // LANES) + h, 1), :], (LANES, LANES)))
            lane = lax.broadcasted_iota(jnp.int32, (LANES, LANES), 1)
            hits = [jnp.where(named == lane + c * LANES, 1.0, 0.0).astype(BF16) for c in range(columns // LANES)]
            parts.append(jnp.concatenate(hits, axis=1))
        tangent[pl.ds(pl.multiple_of(t * tile, tile), tile), :] = dot(
            jnp.concatenate(parts, axis=0), per_column[...]).astype(BF16)
        tangent_copy(t).start()

    def near_group(g):
        lanes = pl.ds(pl.multiple_of(g * LANES, LANES), LANES)
        start, side_at = lon_places(lon, n_lon, across)
        transport_field(lat == 0, lat == n_lat - 1, start, side_at, field, side, near_field, lanes, rates,
                        near_field == 0, window, one, two, n_lon)
        moved[:, :, lanes] = window[pl.ds(HALO, height), pl.ds(start, across), :]

    column_tiles, slot_tiles, groups = columns // tile, slots // tile, levels // LANES
    pl.loop(0, column_tiles // 2)(observe_columns)

    @pl.when(has_near)
    def _():
        take_near_center()
    pl.loop(column_tiles // 2, column_tiles)(observe_columns)

    @pl.when(has_far)
    def _():
        take_far_center()
    pl.loop(0, slot_tiles // 2)(observe_slots)

    @pl.when(has_near)
    def _():
        take_halo(near_field)
    pl.loop(slot_tiles // 2, slot_tiles)(observe_slots)

    @pl.when(has_near)
    def _():
        settle(near_field)

    @pl.loop(0, groups)
    def _(g):
        @pl.when(jnp.logical_and(has_far, g == groups // 2))
        def _():
            take_halo(far_field, True)

        @pl.when(has_near)
        def _():
            near_group(g)

    kept = [pltpu.make_async_copy(moved, moved_out, moved_sem)]
    kept[0].start()

    @pl.when(has_near)
    def _():
        for part in range(2):
            center(far_field, part, {"sub": near}).wait_send()

    @pl.when(near_above)
    def _():
        direct(0).wait_send()

    @pl.when(near_below)
    def _():
        direct(1).wait_send()

    @pl.when(has_far)
    def _():
        settle(far_field)
        for part in range(2):
            center(near_field, part, {"sub": far}).wait_send()
        keep(far_field, 0).wait()

        @pl.when(has_above)
        def _():
            upward(far_field).wait_send()
            keep(far_field, 1).wait()

        @pl.when(has_below)
        def _():
            downward(far_field).wait_send()
            keep(far_field, 2).wait()

    if n_lon > 1:
        kept.append(pltpu.make_async_copy(side.at[far_field], side_out, load_sem.at[0]))
        kept[1].start()
    for item in kept:
        item.wait()
    for t in range(column_tiles):
        adjoint_copy(t).wait()
    for t in range(slot_tiles):
        tangent_copy(t).wait()


def exchange(sizes, count, cols, inc, mul, back, cot, hw, bias, ow, rates):
    height, across, levels = inc.shape
    columns = height * across
    slots, chan = cot.shape
    hid = hw.shape[1]
    total = height + 2 * HALO
    anywhere = pl.BlockSpec(memory_space=pl.ANY)
    vm = pltpu.VMEM
    dma = pltpu.SemaphoreType.DMA
    field_shape, side_shape = (2, total, across, levels), (2, total // 2, 2 * HALO, levels)
    flops = 2 * columns * levels * hid * 5 + 4 * columns * slots * chan
    window, state = transport_scratch(inc.shape, sizes[2])
    return pl.pallas_call(
        functools.partial(exchange_kernel, sizes),
        out_shape=(jax.ShapeDtypeStruct(field_shape[1:], BF16), jax.ShapeDtypeStruct(side_shape[1:], BF16),
                   jax.ShapeDtypeStruct((slots, chan), BF16), jax.ShapeDtypeStruct((columns, levels), F32), jax.ShapeDtypeStruct(inc.shape, F32)),
        in_specs=[pl.BlockSpec(memory_space=pltpu.SMEM)] + [anywhere] * 9,
        out_specs=(anywhere,) * 5,
        scratch_shapes=[
            vm(rates.shape, F32), vm(inc.shape, F32), window, state, state,
            vm(cols.shape, jnp.int32), vm((2,) + inc.shape, F32), vm((2,) + inc.shape, BF16),
            vm(back.shape, BF16), vm(cot.shape, BF16), vm(hw.shape, BF16), vm(bias.shape, F32), vm(ow.shape, BF16),
            vm(field_shape, BF16), vm(side_shape, BF16), vm(side_shape, BF16),
            vm((columns, chan), BF16), vm(cols.shape, jnp.int32), vm((slots, chan), BF16), vm((columns, levels), F32),
            dma((9,)), dma((2, KINDS)), dma((2, KINDS)), dma((3,)), dma((slots // 256,)), dma((columns // 256,)), dma,
        ],
        compiler_params=pltpu.CompilerParams(vmem_limit_bytes=VMEM_BYTES, collective_id=0, has_side_effects=True),
        cost_estimate=pl.CostEstimate(flops=flops, bytes_accessed=20 << 20, transcendentals=columns * hid),
        name="exchange",
    )(count, cols, inc, mul, back, cot, hw, bias, ow, rates)


def lon_places(lon, n_lon, across):
    if n_lon == 1:
        return 0, 0
    first = lon == 0
    return pl.multiple_of(jnp.where(first, 0, HALO), HALO), pl.multiple_of(jnp.where(first, across, 0), HALO)


def transport_scratch(shape, n_lon):
    height, across, _ = shape
    width = (across + (HALO if n_lon > 1 else 0)) // SUB
    total = height + 2 * HALO
    return (pltpu.VMEM((total, width * SUB, LANES), F32),
            pltpu.VMEM((total, width + 2 * REACH, SUB, LANES), F32))


def transport_field(lat_first, lat_last, start, side_at, field, side, f, lanes, rates, is_ahead, window, one, two, n_lon):
    total, width = window.shape[0], window.shape[1] // SUB
    across = field.shape[2]

    @pl.loop(0, total // 2)
    def _(p):
        if n_lon > 1:
            pair = side[f, p, :, lanes].astype(F32)
        for q in range(2):
            window[2 * p + q, pl.ds(start, across), :] = field[f, 2 * p + q, :, lanes].astype(F32)
            if n_lon > 1:
                window[2 * p + q, pl.ds(side_at, HALO), :] = pair[q * HALO:(q + 1) * HALO]

    lane_row = lax.broadcasted_iota(jnp.int32, (SUB, LANES), 0)
    low_edge = lane_row == 0
    high_edge = lane_row == SUB - 1

    def put(ref, r, v, vec):
        ref[r, v + REACH] = vec
        if v >= width - REACH:
            ref[r, v - (width - REACH)] = jnp.where(low_edge, 0.0, pltpu.roll(vec, 1, 0))
        if v < REACH:
            ref[r, v + width + REACH] = jnp.where(high_edge, 0.0, pltpu.roll(vec, SUB - 1, 0))

    def clear_outside(ref):
        zero = jnp.zeros((HALO,) + ref.shape[1:], F32)

        @pl.when(lat_first)
        def _():
            ref[pl.ds(0, HALO)] = zero

        @pl.when(lat_last)
        def _():
            ref[pl.ds(total - HALO, HALO)] = zero

    @pl.loop(0, total // 2)
    def _(p):
        for q in range(2):
            for v in range(width):
                put(one, 2 * p + q, v, window[2 * p + q, pl.ds(v, SUB, stride=width), :])
    clear_outside(one)

    c = [jnp.where(is_ahead, rates[k:k + 1, lanes], rates[m:m + 1, lanes]) for k, m in enumerate((3, 2, 1, 0, 7, 6, 5, 4))]
    c.append(1.0 - (((c[0] + c[1]) + (c[2] + c[3])) + ((c[4] + c[5]) + (c[6] + c[7]))))
    c = [jnp.broadcast_to(x, (SUB, LANES)) for x in c]
    for step in range(STEPS):
        src, dst = (one, two) if step % 2 == 0 else (two, one)
        lo = REACH * (step + 1)

        @pl.loop(0, (total - 2 * lo) // BLOCK)
        def _(b):
            r = lo + b * BLOCK
            lines = [[src[r + q, k] for k in range(2 * REACH)] for q in range(BLOCK)]
            for v in range(width):
                for q in range(BLOCK):
                    lines[q].append(src[r + q, v + 2 * REACH])
                tall = ([src[r + k - REACH, v + REACH] for k in range(REACH)] + [line[v + REACH] for line in lines]
                        + [src[r + BLOCK + k, v + REACH] for k in range(REACH)])
                for q in range(BLOCK):
                    line = lines[q][v:v + 2 * REACH + 1]
                    acc = ((c[8] * tall[q + 2] + c[0] * tall[q]) + (c[1] * tall[q + 1] + c[2] * tall[q + 3])
                           + (c[3] * tall[q + 4] + c[5] * line[1])
                           + ((c[4] * line[0] + c[6] * line[3]) + c[7] * line[4]))
                    if step == STEPS - 1:
                        window[r + q, pl.ds(v, SUB, stride=width), :] = acc
                    else:
                        put(dst, r + q, v, acc)
        if step < STEPS - 1:
            clear_outside(dst)


def transport_kernel(sizes, rates, field, side, moved, inc_ref, mul_ref, adj_ref, err_ref, grad_ref, window, one, two):
    n_sub, n_lat, n_lon = sizes
    sub, lat, lon = lax.axis_index("sub"), lax.axis_index("lat"), lax.axis_index("lon")
    height, across = inc_ref.shape[0], inc_ref.shape[1]
    start, side_at = lon_places(lon, n_lon, across)
    odd = sub % 2
    far_is_ahead = odd == 0
    near = sub + 1 - 2 * odd
    far = sub - 1 + 2 * odd
    result = (pl.ds(HALO, height), pl.ds(start, across))

    @pl.when(jnp.logical_and(far >= 0, far < n_sub))
    def _():
        transport_field(lat == 0, lat == n_lat - 1, start, side_at, field, side, 0, slice(None), rates,
                        far_is_ahead, window, one, two, n_lon)

    @pl.when(jnp.logical_or(far < 0, far >= n_sub))
    def _():
        window[...] = jnp.zeros_like(window)
    near_part = jnp.where(near < n_sub, moved[...], 0.0)
    far_part = window[result]
    err_ref[...] = inc_ref[...] - jnp.where(far_is_ahead, far_part, near_part)
    grad_ref[...] = mul_ref[...] - jnp.where(far_is_ahead, near_part, far_part) + adj_ref[...]


def transport_call(sizes, rates, field, side, moved, inc, mul, adj):
    height, across, levels = inc.shape

    def whole(shape):
        return pl.BlockSpec(shape[:-1] + (LANES,), lambda g: (0,) * (len(shape) - 1) + (g,))
    arrays = (rates, field[None], side[None], moved, inc, mul, adj)
    window, state = transport_scratch(inc.shape, sizes[2])
    return pl.pallas_call(
        functools.partial(transport_kernel, sizes),
        grid=(levels // LANES,),
        out_shape=(jax.ShapeDtypeStruct(inc.shape, F32),) * 2,
        in_specs=[whole(x.shape) for x in arrays],
        out_specs=(whole(inc.shape),) * 2,
        scratch_shapes=[window, state, state],
        compiler_params=pltpu.CompilerParams(vmem_limit_bytes=VMEM_BYTES),
        cost_estimate=pl.CostEstimate(flops=4 * 17 * height * across * levels, bytes_accessed=16 << 20, transcendentals=0),
        name="transport",
    )(*arrays)


def local(increment, multiplier, background, obs_cotangent, obs_column, obs_count, transport,
          hidden_weight, hidden_bias, output_weight):
    sizes = tuple(lax.axis_size(name) for name in ("sub", "lat", "lon"))
    assert sizes[2] <= 2
    inc, mul = increment[0], multiplier[0]
    levels = inc.shape[-1]
    field, side, tangent, adj, moved = exchange(
        sizes, obs_count[0], obs_column.reshape(-1, LANES), inc, mul, background.reshape(-1, levels),
        obs_cotangent[0, 0], hidden_weight, hidden_bias[None], output_weight, transport)
    err, grad = transport_call(sizes, transport, field, side, moved, inc, mul, adj.reshape(inc.shape))
    return err[None], grad[None], tangent[None, None]


def solution(mesh):
    field = P("sub", "lat", "lon", None)
    slots = P("sub", ("lat", "lon"), None, None)
    in_specs = (field, field, field, slots, P("sub", ("lat", "lon"), None), P("sub", None), P(), P(), P(), P())
    return jax.shard_map(local, mesh=mesh, in_specs=in_specs, out_specs=(field, field, slots), check_vma=False)
```

time: 65.3 us -> 51.3 us (0.79)
  local copies, waits for them, and re-layouts: 9.96 us -> 1.33 us
  Pallas kernels: 52.4 us -> 49.1 us
  other arithmetic: 1.47 us -> 0 us
    pallas_call x1, Pallas kernels: 22.3 us -> 13.4 us  [transport_call(): pl.pallas_call(functools.partial(transport_kernel, sizes), grid=(levels /...]
    unnamed x19 -> x3, local copies, waits for them, and re-layouts: 8.35 us -> 1.33 us
    pallas_call x1, Pallas kernels: 30.1 us -> 35.7 us  [exchange(): pl.pallas_call(functools.partial(exchange_kernel, sizes), out_shape=(jax....]
    slice x1 -> x0, local copies, waits for them, and re-layouts: 0.8 us -> none  [local(): wm = jnp.concatenate([transport[3::-1], transport[7:3:-1], rest], axis=0)]
    reduce_sum x1 -> x0, other arithmetic: 0.73 us -> none  [local(): rest = (1.0 - jnp.sum(transport, axis=0))[None]]
    concatenate x1 -> x0, other arithmetic: 0.73 us -> none  [local(): wm = jnp.concatenate([transport[3::-1], transport[7:3:-1], rest], axis=0)]
where the time goes in v3:
time: 51.3 us; the launch traced here: 51 us
  Pallas kernels  49.1 us (96%)
  local copies, waits for them, and re-layouts  1.33 us (3%)
  between operations  0.65 us (1%)
    pallas_call x1, Pallas kernels, exchange(): pl.pallas_call(functools.partial(exchange_kernel, sizes), out_shape=(jax....  35.7 us
    pallas_call x1, Pallas kernels, transport_call(): pl.pallas_call(functools.partial(transport_kernel, sizes), grid=(levels /...  13.4 us
    unnamed x3, local copies, waits for them, and re-layouts  1.33 us

profile of v3, /device:TPU:1, one launch (start us, length us, event | category | flops | bytes accessed | tf_op | source)
XLA Modules:
  0.0 51.0 jit_solution(2277735399289942283)
XLA Ops:
  0.6 35.7 %exchange.1 = (bf16[32,64,512]{2,1,0:T(8,128)(2,1)}, bf16[16,16,512]{2,1,0:T(8,128)(2,1)}, bf16[2048,512]{1,0:T(8,128)(2,1)}, f32[1024,512]{1,0:T(8,128)}, f32[16,64,512]{2,1,0:T(8,128)}) custom-call(s32[8]{0:T(128)} %bitcast.27, s32[16,128]{1,0:T(8,128)} %bitcast.25, f32[16,64,512]{2,1,0:T(8,128)} %bitcast.14, f32[16,64,512]{2,1,0:T(8,128)} %bitcast.16, ...), custom_call_target="tpu_custom_call" | custom-call | flops 9663676416 | bytes 20971520 | tf_op jit(solution)/shard_map/exchange/pallas_call | solution.py:326
  36.3 0.0 copy-start
  36.3 13.4 %transport.1 = (f32[16,64,512]{2,1,0:T(8,128)}, f32[16,64,512]{2,1,0:T(8,128)}) custom-call(f32[8,512]{1,0:T(8,128)} %rates.1, bf16[1,32,64,512]{3,2,1,0:T(8,128)(2,1)} %bitcast.18, bf16[1,16,16,512]{3,2,1,0:T(8,128)(2,1)} %bitcast.20, f32[16,64,512]{2,1,0:T(8,128)} %get-tuple-element.12.moved, f32[16,64,512]{2,1,0:T(8,128)} %bitcast.15, ...), custom_call_target="tpu_custom_call" | custom-call | flops 35651584 | bytes 16777216 | tf_op jit(solution)/shard_map/transport/pallas_call | solution.py:464
  49.7 0.0 copy-done
  49.7 1.3 %copy.14 = bf16[1,1,2048,512]{3,2,1,0:T(8,128)(2,1)} copy(bf16[1,1,2048,512]{3,2,1,0:T(8,128)(2,1)S(1)} %bitcast.13) | data formatting | bytes 4194304
Async XLA Ops:
  36.3 13.4 %copy-start = (bf16[2048,512]{1,0:T(8,128)(2,1)S(1)}, bf16[2048,512]{1,0:T(8,128)(2,1)}, u32[]{:S(2)}) copy-start(bf16[2048,512]{1,0:T(8,128)(2,1)} %get-tuple-element.16) | copy-start | bytes 6291460

commit v4 on v3

--- a/solution.py
+++ b/solution.py
@@ -12,6 +12,9 @@
 HALO = STEPS * REACH
 SUB = 8
 LANES = 128
+PAIR = 2
+TILE = 512
+WIDE = PAIR * LANES
 BLOCK = 4
 MESH = pl.DeviceIdType.MESH
 NT = (((1,), (1,)), ((), ()))
@@ -156,11 +159,14 @@
                 sideways(f, 2).wait()
 
     def cast(f):
-        pltpu.make_async_copy(inc_hbm, raw.at[f], load_sem.at[f]).wait()
         for part in range(2):
             rows = pl.ds(part * HALO, HALO)
             sent[f, rows] = raw[f, rows].astype(BF16)
 
+    for load in loads[:2]:
+        load.wait()
+    for load in loads[2:]:
+        load.start()
     cast(near_field)
     pl.semaphore_wait(barrier, amount)
 
@@ -184,11 +190,9 @@
             center(far_field, part, {"sub": near}).start()
 
     for load in loads[2:]:
-        load.start()
-    for load in loads[2:]:
         load.wait()
     count = count_ref[lat * n_lon + lon]
-    tile = 256
+    tile = TILE
     chunks = slots // LANES
     place = (lax.broadcasted_iota(jnp.int32, (chunks, LANES), 0) * LANES
              + lax.broadcasted_iota(jnp.int32, (chunks, LANES), 1))
@@ -229,13 +233,14 @@
         tangent_copy(t).start()
 
     def near_group(g):
-        lanes = pl.ds(pl.multiple_of(g * LANES, LANES), LANES)
+        lanes = [pl.ds(pl.multiple_of(g * WIDE + h * LANES, LANES), LANES) for h in range(PAIR)]
         start, side_at = lon_places(lon, n_lon, across)
         transport_field(lat == 0, lat == n_lat - 1, start, side_at, field, side, near_field, lanes, rates,
                         near_field == 0, window, one, two, n_lon)
-        moved[:, :, lanes] = window[pl.ds(HALO, height), pl.ds(start, across), :]
-
-    column_tiles, slot_tiles, groups = columns // tile, slots // tile, levels // LANES
+        for h in range(PAIR):
+            moved[:, :, lanes[h]] = window[h, pl.ds(HALO, height), pl.ds(start, across), :]
+
+    column_tiles, slot_tiles, groups = columns // tile, slots // tile, levels // WIDE
     pl.loop(0, column_tiles // 2)(observe_columns)
 
     @pl.when(has_near)
@@ -335,7 +340,7 @@
             vm(back.shape, BF16), vm(cot.shape, BF16), vm(hw.shape, BF16), vm(bias.shape, F32), vm(ow.shape, BF16),
             vm(field_shape, BF16), vm(side_shape, BF16), vm(side_shape, BF16),
             vm((columns, chan), BF16), vm(cols.shape, jnp.int32), vm((slots, chan), BF16), vm((columns, levels), F32),
-            dma((9,)), dma((2, KINDS)), dma((2, KINDS)), dma((3,)), dma((slots // 256,)), dma((columns // 256,)), dma,
+            dma((9,)), dma((2, KINDS)), dma((2, KINDS)), dma((3,)), dma((slots // TILE,)), dma((columns // TILE,)), dma,
         ],
         compiler_params=pltpu.CompilerParams(vmem_limit_bytes=VMEM_BYTES, collective_id=0, has_side_effects=True),
         cost_estimate=pl.CostEstimate(flops=flops, bytes_accessed=20 << 20, transcendentals=columns * hid),
@@ -354,82 +359,97 @@
     height, across, _ = shape
     width = (across + (HALO if n_lon > 1 else 0)) // SUB
     total = height + 2 * HALO
-    return (pltpu.VMEM((total, width * SUB, LANES), F32),
-            pltpu.VMEM((total, width + 2 * REACH, SUB, LANES), F32))
+    return (pltpu.VMEM((PAIR, total, width * SUB, LANES), F32),
+            pltpu.VMEM((PAIR, total, width + 2 * REACH, SUB, LANES), F32))
 
 
 def transport_field(lat_first, lat_last, start, side_at, field, side, f, lanes, rates, is_ahead, window, one, two, n_lon):
-    total, width = window.shape[0], window.shape[1] // SUB
+    total, width = window.shape[1], window.shape[2] // SUB
     across = field.shape[2]
-
-    @pl.loop(0, total // 2)
-    def _(p):
-        if n_lon > 1:
-            pair = side[f, p, :, lanes].astype(F32)
-        for q in range(2):
-            window[2 * p + q, pl.ds(start, across), :] = field[f, 2 * p + q, :, lanes].astype(F32)
-            if n_lon > 1:
-                window[2 * p + q, pl.ds(side_at, HALO), :] = pair[q * HALO:(q + 1) * HALO]
-
     lane_row = lax.broadcasted_iota(jnp.int32, (SUB, LANES), 0)
     low_edge = lane_row == 0
     high_edge = lane_row == SUB - 1
 
-    def put(ref, r, v, vec):
-        ref[r, v + REACH] = vec
+    def put(ref, h, r, v, vec):
+        ref[h, r, v + REACH] = vec
         if v >= width - REACH:
-            ref[r, v - (width - REACH)] = jnp.where(low_edge, 0.0, pltpu.roll(vec, 1, 0))
+            ref[h, r, v - (width - REACH)] = jnp.where(low_edge, 0.0, pltpu.roll(vec, 1, 0))
         if v < REACH:
-            ref[r, v + width + REACH] = jnp.where(high_edge, 0.0, pltpu.roll(vec, SUB - 1, 0))
+            ref[h, r, v + width + REACH] = jnp.where(high_edge, 0.0, pltpu.roll(vec, SUB - 1, 0))
 
     def clear_outside(ref):
-        zero = jnp.zeros((HALO,) + ref.shape[1:], F32)
+        zero = jnp.zeros((PAIR, HALO) + ref.shape[2:], F32)
 
         @pl.when(lat_first)
         def _():
-            ref[pl.ds(0, HALO)] = zero
+            ref[:, pl.ds(0, HALO)] = zero
 
         @pl.when(lat_last)
         def _():
-            ref[pl.ds(total - HALO, HALO)] = zero
+            ref[:, pl.ds(total - HALO, HALO)] = zero
+
+    def fill(h, p):
+        if n_lon > 1:
+            pair = side[f, p, :, lanes[h]].astype(F32)
+        for q in range(2):
+            window[h, 2 * p + q, pl.ds(start, across), :] = field[f, 2 * p + q, :, lanes[h]].astype(F32)
+            if n_lon > 1:
+                window[h, 2 * p + q, pl.ds(side_at, HALO), :] = pair[q * HALO:(q + 1) * HALO]
 
     @pl.loop(0, total // 2)
     def _(p):
-        for q in range(2):
-            for v in range(width):
-                put(one, 2 * p + q, v, window[2 * p + q, pl.ds(v, SUB, stride=width), :])
+        for h in range(PAIR):
+            fill(h, p)
+
+    @pl.loop(0, total // 2)
+    def _(p):
+        for h in range(PAIR):
+            for q in range(2):
+                for v in range(width):
+                    put(one, h, 2 * p + q, v, window[h, 2 * p + q, pl.ds(v, SUB, stride=width), :])
     clear_outside(one)
 
-    c = [jnp.where(is_ahead, rates[k:k + 1, lanes], rates[m:m + 1, lanes]) for k, m in enumerate((3, 2, 1, 0, 7, 6, 5, 4))]
-    c.append(1.0 - (((c[0] + c[1]) + (c[2] + c[3])) + ((c[4] + c[5]) + (c[6] + c[7]))))
-    c = [jnp.broadcast_to(x, (SUB, LANES)) for x in c]
+    coeffs = []
+    for h in range(PAIR):
+        c = [jnp.where(is_ahead, rates[k:k + 1, lanes[h]], rates[m:m + 1, lanes[h]])
+             for k, m in enumerate((3, 2, 1, 0, 7, 6, 5, 4))]
+        rest = 1.0 - (((c[0] + c[1]) + (c[2] + c[3])) + ((c[4] + c[5]) + (c[6] + c[7])))
+        scale = 1.0 / rest
+        square = rest * rest
+        coeffs.append([jnp.broadcast_to(x, (SUB, LANES)) for x in [x * scale for x in c] + [square * square]])
+
+    def advance(src, dst, h, r, last):
+        c = coeffs[h]
+        lines = [[src[h, r + q, k] for k in range(2 * REACH)] for q in range(BLOCK)]
+        for v in range(width):
+            for q in range(BLOCK):
+                lines[q].append(src[h, r + q, v + 2 * REACH])
+            tall = ([src[h, r + k - REACH, v + REACH] for k in range(REACH)] + [line[v + REACH] for line in lines]
+                    + [src[h, r + BLOCK + k, v + REACH] for k in range(REACH)])
+            for q in range(BLOCK):
+                line = lines[q][v:v + 2 * REACH + 1]
+                acc = ((tall[q + 2] + c[0] * tall[q]) + (c[1] * tall[q + 1] + c[2] * tall[q + 3])
+                       + (c[3] * tall[q + 4] + c[5] * line[1])
+                       + ((c[4] * line[0] + c[6] * line[3]) + c[7] * line[4]))
+                if last:
+                    window[h, r + q, pl.ds(v, SUB, stride=width), :] = acc * c[8]
+                else:
+                    put(dst, h, r + q, v, acc)
+
     for step in range(STEPS):
         src, dst = (one, two) if step % 2 == 0 else (two, one)
         lo = REACH * (step + 1)
 
         @pl.loop(0, (total - 2 * lo) // BLOCK)
         def _(b):
-            r = lo + b * BLOCK
-            lines = [[src[r + q, k] for k in range(2 * REACH)] for q in range(BLOCK)]
-            for v in range(width):
-                for q in range(BLOCK):
-                    lines[q].append(src[r + q, v + 2 * REACH])
-                tall = ([src[r + k - REACH, v + REACH] for k in range(REACH)] + [line[v + REACH] for line in lines]
-                        + [src[r + BLOCK + k, v + REACH] for k in range(REACH)])
-                for q in range(BLOCK):
-                    line = lines[q][v:v + 2 * REACH + 1]
-                    acc = ((c[8] * tall[q + 2] + c[0] * tall[q]) + (c[1] * tall[q + 1] + c[2] * tall[q + 3])
-                           + (c[3] * tall[q + 4] + c[5] * line[1])
-                           + ((c[4] * line[0] + c[6] * line[3]) + c[7] * line[4]))
-                    if step == STEPS - 1:
-                        window[r + q, pl.ds(v, SUB, stride=width), :] = acc
-                    else:
-                        put(dst, r + q, v, acc)
+            for h in range(PAIR):
+                advance(src, dst, h, lo + b * BLOCK, step == STEPS - 1)
         if step < STEPS - 1:
             clear_outside(dst)
 
 
-def transport_kernel(sizes, rates, field, side, moved, inc_ref, mul_ref, adj_ref, err_ref, grad_ref, window, one, two):
+def transport_kernel(sizes, rates, field, side, moved, inc_ref, mul_ref, adj_ref, tangent, err_ref, grad_ref, tangent_out,
+                     window, one, two, tan_sem):
     n_sub, n_lat, n_lon = sizes
     sub, lat, lon = lax.axis_index("sub"), lax.axis_index("lat"), lax.axis_index("lon")
     height, across = inc_ref.shape[0], inc_ref.shape[1]
@@ -439,39 +459,52 @@
     near = sub + 1 - 2 * odd
     far = sub - 1 + 2 * odd
     result = (pl.ds(HALO, height), pl.ds(start, across))
+    lanes = [slice(h * LANES, (h + 1) * LANES) for h in range(PAIR)]
+    tangent_copy = pltpu.make_async_copy(tangent, tangent_out, tan_sem)
+
+    @pl.when(pl.program_id(0) == 0)
+    def _():
+        tangent_copy.start()
 
     @pl.when(jnp.logical_and(far >= 0, far < n_sub))
     def _():
-        transport_field(lat == 0, lat == n_lat - 1, start, side_at, field, side, 0, slice(None), rates,
+        transport_field(lat == 0, lat == n_lat - 1, start, side_at, field, side, 0, lanes, rates,
                         far_is_ahead, window, one, two, n_lon)
 
     @pl.when(jnp.logical_or(far < 0, far >= n_sub))
     def _():
         window[...] = jnp.zeros_like(window)
-    near_part = jnp.where(near < n_sub, moved[...], 0.0)
-    far_part = window[result]
-    err_ref[...] = inc_ref[...] - jnp.where(far_is_ahead, far_part, near_part)
-    grad_ref[...] = mul_ref[...] - jnp.where(far_is_ahead, near_part, far_part) + adj_ref[...]
-
-
-def transport_call(sizes, rates, field, side, moved, inc, mul, adj):
+    for h in range(PAIR):
+        part = (slice(None), slice(None), lanes[h])
+        near_part = jnp.where(near < n_sub, moved[part], 0.0)
+        far_part = window[(h,) + result]
+        err_ref[part] = inc_ref[part] - jnp.where(far_is_ahead, far_part, near_part)
+        grad_ref[part] = mul_ref[part] - jnp.where(far_is_ahead, near_part, far_part) + adj_ref[part]
+
+    @pl.when(pl.program_id(0) == pl.num_programs(0) - 1)
+    def _():
+        tangent_copy.wait()
+
+
+def transport_call(sizes, rates, field, side, moved, inc, mul, adj, tangent):
     height, across, levels = inc.shape
 
     def whole(shape):
-        return pl.BlockSpec(shape[:-1] + (LANES,), lambda g: (0,) * (len(shape) - 1) + (g,))
+        return pl.BlockSpec(shape[:-1] + (WIDE,), lambda g: (0,) * (len(shape) - 1) + (g,))
+    anywhere = pl.BlockSpec(memory_space=pl.ANY)
     arrays = (rates, field[None], side[None], moved, inc, mul, adj)
     window, state = transport_scratch(inc.shape, sizes[2])
     return pl.pallas_call(
         functools.partial(transport_kernel, sizes),
-        grid=(levels // LANES,),
-        out_shape=(jax.ShapeDtypeStruct(inc.shape, F32),) * 2,
-        in_specs=[whole(x.shape) for x in arrays],
-        out_specs=(whole(inc.shape),) * 2,
-        scratch_shapes=[window, state, state],
+        grid=(levels // WIDE,),
+        out_shape=(jax.ShapeDtypeStruct(inc.shape, F32),) * 2 + (jax.ShapeDtypeStruct(tangent.shape, BF16),),
+        in_specs=[whole(x.shape) for x in arrays] + [anywhere],
+        out_specs=(whole(inc.shape),) * 2 + (anywhere,),
+        scratch_shapes=[window, state, state, pltpu.SemaphoreType.DMA],
         compiler_params=pltpu.CompilerParams(vmem_limit_bytes=VMEM_BYTES),
         cost_estimate=pl.CostEstimate(flops=4 * 17 * height * across * levels, bytes_accessed=16 << 20, transcendentals=0),
         name="transport",
-    )(*arrays)
+    )(*arrays, tangent)
 
 
 def local(increment, multiplier, background, obs_cotangent, obs_column, obs_count, transport,
@@ -483,7 +516,7 @@
     field, side, tangent, adj, moved = exchange(
         sizes, obs_count[0], obs_column.reshape(-1, LANES), inc, mul, background.reshape(-1, levels),
         obs_cotangent[0, 0], hidden_weight, hidden_bias[None], output_weight, transport)
-    err, grad = transport_call(sizes, transport, field, side, moved, inc, mul, adj.reshape(inc.shape))
+    err, grad, tangent = transport_call(sizes, transport, field, side, moved, inc, mul, adj.reshape(inc.shape), tangent)
     return err[None], grad[None], tangent[None, None]
 
 

time: 51.3 us -> 103 us (2.01)
  Pallas kernels: 49.1 us -> 103 us
  local copies, waits for them, and re-layouts: 1.33 us -> 0 us
    pallas_call x1, Pallas kernels: 13.4 us -> 68.5 us  [transport_call(): pl.pallas_call(functools.partial(transport_kernel, sizes), grid=(levels /...]
    pallas_call x1, Pallas kernels: 35.7 us -> 34 us  [exchange(): pl.pallas_call(functools.partial(exchange_kernel, sizes), out_shape=(jax....]
    unnamed x3 -> x0, local copies, waits for them, and re-layouts: 1.33 us -> none
where the time goes in v4:
time: 103 us
  Pallas kernels  103 us (100%)
    pallas_call x1, Pallas kernels, transport_call(): pl.pallas_call(functools.partial(transport_kernel, sizes), grid=(levels /...  68.5 us
    pallas_call x1, Pallas kernels, exchange(): pl.pallas_call(functools.partial(exchange_kernel, sizes), out_shape=(jax....  34 us

profile of v4, /device:TPU:1, one launch (start us, length us, event | category | flops | bytes accessed | tf_op | source)
XLA Modules:
  0.0 103.2 jit_solution(4619601125979257501)
XLA Ops:
  0.6 34.0 %exchange.1 = (bf16[32,64,512]{2,1,0:T(8,128)(2,1)}, bf16[16,16,512]{2,1,0:T(8,128)(2,1)}, bf16[2048,512]{1,0:T(8,128)(2,1)}, f32[1024,512]{1,0:T(8,128)}, f32[16,64,512]{2,1,0:T(8,128)}) custom-call(s32[8]{0:T(128)} %bitcast.27, s32[16,128]{1,0:T(8,128)} %bitcast.25, f32[16,64,512]{2,1,0:T(8,128)} %bitcast.13, f32[16,64,512]{2,1,0:T(8,128)} %bitcast.15, ...), custom_call_target="tpu_custom_call" | custom-call | flops 9663676416 | bytes 20971520 | tf_op jit(solution)/shard_map/exchange/pallas_call | solution.py:331
  34.6 68.5 %transport.1 = (f32[16,64,512]{2,1,0:T(8,128)}, f32[16,64,512]{2,1,0:T(8,128)}, bf16[2048,512]{1,0:T(8,128)(2,1)}) custom-call(f32[8,512]{1,0:T(8,128)} %rates.1, bf16[1,32,64,512]{3,2,1,0:T(8,128)(2,1)} %bitcast.17, bf16[1,16,16,512]{3,2,1,0:T(8,128)(2,1)} %bitcast.19, f32[16,64,512]{2,1,0:T(8,128)} %get-tuple-element.13.moved, f32[16,64,512]{2,1,0:T(8,128)} %bitcast.14, ...), custom_call_target="tpu_custom_call" | custom-call | flops 35651584 | bytes 16777216 | tf_op jit(solution)/shard_map/transport/pallas_call | solution.py:497

commit v5 on v4

--- a/solution.py
+++ b/solution.py
@@ -122,12 +122,14 @@
         center(near_field, 1, {"sub": near}).wait_recv()
         pass_on(near_field, 0)
 
-    def take_far_center():
+    def take_far_upper():
         center(far_field, 0, {"sub": far}).wait_recv()
 
         @pl.when(has_above)
         def _():
             upward(far_field).start()
+
+    def take_far_lower():
         center(far_field, 1, {"sub": far}).wait_recv()
 
         @pl.when(has_below)
@@ -250,13 +252,16 @@
 
     @pl.when(has_far)
     def _():
-        take_far_center()
-    pl.loop(0, slot_tiles // 2)(observe_slots)
+        take_far_upper()
+    pl.loop(0, slot_tiles)(observe_slots)
 
     @pl.when(has_near)
     def _():
         take_halo(near_field)
-    pl.loop(slot_tiles // 2, slot_tiles)(observe_slots)
+
+    @pl.when(has_far)
+    def _():
+        take_far_lower()
 
     @pl.when(has_near)
     def _():
@@ -449,7 +454,7 @@
 
 
 def transport_kernel(sizes, rates, field, side, moved, inc_ref, mul_ref, adj_ref, tangent, err_ref, grad_ref, tangent_out,
-                     window, one, two, tan_sem):
+                     window, one, two):
     n_sub, n_lat, n_lon = sizes
     sub, lat, lon = lax.axis_index("sub"), lax.axis_index("lat"), lax.axis_index("lon")
     height, across = inc_ref.shape[0], inc_ref.shape[1]
@@ -460,11 +465,7 @@
     far = sub - 1 + 2 * odd
     result = (pl.ds(HALO, height), pl.ds(start, across))
     lanes = [slice(h * LANES, (h + 1) * LANES) for h in range(PAIR)]
-    tangent_copy = pltpu.make_async_copy(tangent, tangent_out, tan_sem)
-
-    @pl.when(pl.program_id(0) == 0)
-    def _():
-        tangent_copy.start()
+    tangent_out[...] = tangent[...]
 
     @pl.when(jnp.logical_and(far >= 0, far < n_sub))
     def _():
@@ -481,26 +482,21 @@
         err_ref[part] = inc_ref[part] - jnp.where(far_is_ahead, far_part, near_part)
         grad_ref[part] = mul_ref[part] - jnp.where(far_is_ahead, near_part, far_part) + adj_ref[part]
 
-    @pl.when(pl.program_id(0) == pl.num_programs(0) - 1)
-    def _():
-        tangent_copy.wait()
-
-
 def transport_call(sizes, rates, field, side, moved, inc, mul, adj, tangent):
     height, across, levels = inc.shape
 
     def whole(shape):
         return pl.BlockSpec(shape[:-1] + (WIDE,), lambda g: (0,) * (len(shape) - 1) + (g,))
-    anywhere = pl.BlockSpec(memory_space=pl.ANY)
+    part = pl.BlockSpec((tangent.shape[0] * WIDE // levels, tangent.shape[1]), lambda g: (g, 0))
     arrays = (rates, field[None], side[None], moved, inc, mul, adj)
     window, state = transport_scratch(inc.shape, sizes[2])
     return pl.pallas_call(
         functools.partial(transport_kernel, sizes),
         grid=(levels // WIDE,),
         out_shape=(jax.ShapeDtypeStruct(inc.shape, F32),) * 2 + (jax.ShapeDtypeStruct(tangent.shape, BF16),),
-        in_specs=[whole(x.shape) for x in arrays] + [anywhere],
-        out_specs=(whole(inc.shape),) * 2 + (anywhere,),
-        scratch_shapes=[window, state, state, pltpu.SemaphoreType.DMA],
+        in_specs=[whole(x.shape) for x in arrays] + [part],
+        out_specs=(whole(inc.shape),) * 2 + (part,),
+        scratch_shapes=[window, state, state],
         compiler_params=pltpu.CompilerParams(vmem_limit_bytes=VMEM_BYTES),
         cost_estimate=pl.CostEstimate(flops=4 * 17 * height * across * levels, bytes_accessed=16 << 20, transcendentals=0),
         name="transport",

time: 103 us -> 48.5 us (0.47)
  Pallas kernels: 103 us -> 47.7 us
    pallas_call x1, Pallas kernels: 68.5 us -> 14.4 us  [transport_call(): pl.pallas_call(functools.partial(transport_kernel, sizes), grid=(levels /...]
where the time goes in v5:
time: 48.5 us; the launch traced here: 48.3 us
  Pallas kernels  47.7 us (98%)
  between operations  0.64 us (1%)
    pallas_call x1, Pallas kernels, exchange(): pl.pallas_call(functools.partial(exchange_kernel, sizes), out_shape=(jax....  33.3 us
    pallas_call x1, Pallas kernels, transport_call(): pl.pallas_call(functools.partial(transport_kernel, sizes), grid=(levels /...  14.4 us

profile of v5, /device:TPU:1, one launch (start us, length us, event | category | flops | bytes accessed | tf_op | source)
XLA Modules:
  0.0 48.3 jit_solution(4807356638793813836)
XLA Ops:
  0.6 33.3 %exchange.1 = (bf16[32,64,512]{2,1,0:T(8,128)(2,1)}, bf16[16,16,512]{2,1,0:T(8,128)(2,1)}, bf16[2048,512]{1,0:T(8,128)(2,1)}, f32[1024,512]{1,0:T(8,128)}, f32[16,64,512]{2,1,0:T(8,128)}) custom-call(s32[8]{0:T(128)} %bitcast.27, s32[16,128]{1,0:T(8,128)} %bitcast.25, f32[16,64,512]{2,1,0:T(8,128)} %bitcast.13, f32[16,64,512]{2,1,0:T(8,128)} %bitcast.15, ...), custom_call_target="tpu_custom_call" | custom-call | flops 9663676416 | bytes 20971520 | tf_op jit(solution)/shard_map/exchange/pallas_call | solution.py:336
  34.0 14.4 %transport.1 = (f32[16,64,512]{2,1,0:T(8,128)}, f32[16,64,512]{2,1,0:T(8,128)}, bf16[2048,512]{1,0:T(8,128)(2,1)}) custom-call(f32[8,512]{1,0:T(8,128)} %rates.1, bf16[1,32,64,512]{3,2,1,0:T(8,128)(2,1)} %bitcast.17, bf16[1,16,16,512]{3,2,1,0:T(8,128)(2,1)} %bitcast.19, f32[16,64,512]{2,1,0:T(8,128)} %get-tuple-element.13.moved, f32[16,64,512]{2,1,0:T(8,128)} %bitcast.14, ...), custom_call_target="tpu_custom_call" | custom-call | flops 35651584 | bytes 16777216 | tf_op jit(solution)/shard_map/transport/pallas_call | solution.py:493

commit v6 on v5

--- a/solution.py
+++ b/solution.py
@@ -242,6 +242,10 @@
         for h in range(PAIR):
             moved[:, :, lanes[h]] = window[h, pl.ds(HALO, height), pl.ds(start, across), :]
 
+    def moved_copy(g):
+        lanes = pl.ds(pl.multiple_of(g * WIDE, WIDE), WIDE)
+        return pltpu.make_async_copy(moved.at[:, :, lanes], moved_out.at[:, :, lanes], moved_sem.at[g])
+
     column_tiles, slot_tiles, groups = columns // tile, slots // tile, levels // WIDE
     pl.loop(0, column_tiles // 2)(observe_columns)
 
@@ -276,12 +280,14 @@
         @pl.when(has_near)
         def _():
             near_group(g)
-
-    kept = [pltpu.make_async_copy(moved, moved_out, moved_sem)]
-    kept[0].start()
+            moved_copy(g).start()
+
+    kept = []
 
     @pl.when(has_near)
     def _():
+        for g in range(groups):
+            moved_copy(g).wait()
         for part in range(2):
             center(far_field, part, {"sub": near}).wait_send()
 
@@ -312,7 +318,7 @@
 
     if n_lon > 1:
         kept.append(pltpu.make_async_copy(side.at[far_field], side_out, load_sem.at[0]))
-        kept[1].start()
+        kept[0].start()
     for item in kept:
         item.wait()
     for t in range(column_tiles):
@@ -345,7 +351,7 @@
             vm(back.shape, BF16), vm(cot.shape, BF16), vm(hw.shape, BF16), vm(bias.shape, F32), vm(ow.shape, BF16),
             vm(field_shape, BF16), vm(side_shape, BF16), vm(side_shape, BF16),
             vm((columns, chan), BF16), vm(cols.shape, jnp.int32), vm((slots, chan), BF16), vm((columns, levels), F32),
-            dma((9,)), dma((2, KINDS)), dma((2, KINDS)), dma((3,)), dma((slots // TILE,)), dma((columns // TILE,)), dma,
+            dma((9,)), dma((2, KINDS)), dma((2, KINDS)), dma((3,)), dma((slots // TILE,)), dma((columns // TILE,)), dma((levels // WIDE,)),
         ],
         compiler_params=pltpu.CompilerParams(vmem_limit_bytes=VMEM_BYTES, collective_id=0, has_side_effects=True),
         cost_estimate=pl.CostEstimate(flops=flops, bytes_accessed=20 << 20, transcendentals=columns * hid),
@@ -453,54 +459,95 @@
             clear_outside(dst)
 
 
-def transport_kernel(sizes, rates, field, side, moved, inc_ref, mul_ref, adj_ref, tangent, err_ref, grad_ref, tangent_out,
-                     window, one, two):
+def transport_kernel(sizes, rates_hbm, field_hbm, side_hbm, moved_hbm, inc_hbm, mul_hbm, adj_hbm, tangent_hbm,
+                     err_hbm, grad_hbm, tangent_out,
+                     rates, field, side, moved, inc, mul, adj, tangent, err, grad, window, one, two,
+                     field_sem, load_sem, err_sem, grad_sem, tangent_sem):
     n_sub, n_lat, n_lon = sizes
     sub, lat, lon = lax.axis_index("sub"), lax.axis_index("lat"), lax.axis_index("lon")
-    height, across = inc_ref.shape[0], inc_ref.shape[1]
+    height, across, levels = inc.shape
     start, side_at = lon_places(lon, n_lon, across)
     odd = sub % 2
     far_is_ahead = odd == 0
     near = sub + 1 - 2 * odd
     far = sub - 1 + 2 * odd
+    has_far = jnp.logical_and(far >= 0, far < n_sub)
     result = (pl.ds(HALO, height), pl.ds(start, across))
-    lanes = [slice(h * LANES, (h + 1) * LANES) for h in range(PAIR)]
-    tangent_out[...] = tangent[...]
-
-    @pl.when(jnp.logical_and(far >= 0, far < n_sub))
-    def _():
-        transport_field(lat == 0, lat == n_lat - 1, start, side_at, field, side, 0, lanes, rates,
-                        far_is_ahead, window, one, two, n_lon)
-
-    @pl.when(jnp.logical_or(far < 0, far >= n_sub))
-    def _():
-        window[...] = jnp.zeros_like(window)
-    for h in range(PAIR):
-        part = (slice(None), slice(None), lanes[h])
-        near_part = jnp.where(near < n_sub, moved[part], 0.0)
-        far_part = window[(h,) + result]
-        err_ref[part] = inc_ref[part] - jnp.where(far_is_ahead, far_part, near_part)
-        grad_ref[part] = mul_ref[part] - jnp.where(far_is_ahead, near_part, far_part) + adj_ref[part]
+    groups = levels // WIDE
+
+    def field_load(g):
+        lanes = pl.ds(pl.multiple_of(g * WIDE, WIDE), WIDE)
+        return pltpu.make_async_copy(field_hbm.at[:, :, :, lanes], field.at[:, :, :, lanes], field_sem.at[g])
+
+    def store(src, dst, sem, g):
+        lanes = pl.ds(pl.multiple_of(g * WIDE, WIDE), WIDE)
+        return pltpu.make_async_copy(src.at[:, :, lanes], dst.at[:, :, lanes], sem.at[g])
+
+    pairs = [(rates_hbm, rates), (side_hbm, side), (inc_hbm, inc), (moved_hbm, moved), (mul_hbm, mul), (adj_hbm, adj),
+             (tangent_hbm, tangent)]
+    loads = [pltpu.make_async_copy(x, y, load_sem.at[k]) for k, (x, y) in enumerate(pairs)]
+    keep_tangent = pltpu.make_async_copy(tangent, tangent_out, tangent_sem)
+    for load in loads[:2]:
+        load.start()
+    for g in range(groups):
+        field_load(g).start()
+    for load in loads[2:]:
+        load.start()
+    for load in loads[:2]:
+        load.wait()
+
+    @pl.loop(0, groups)
+    def _(g):
+        lanes = [pl.ds(pl.multiple_of(g * WIDE + h * LANES, LANES), LANES) for h in range(PAIR)]
+        field_load(g).wait()
+
+        @pl.when(has_far)
+        def _():
+            transport_field(lat == 0, lat == n_lat - 1, start, side_at, field, side, 0, lanes, rates,
+                            far_is_ahead, window, one, two, n_lon)
+
+        @pl.when(jnp.logical_not(has_far))
+        def _():
+            window[...] = jnp.zeros_like(window)
+
+        @pl.when(g == 0)
+        def _():
+            for load in loads[2:]:
+                load.wait()
+            keep_tangent.start()
+        for h in range(PAIR):
+            part = (slice(None), slice(None), lanes[h])
+            near_part = jnp.where(near < n_sub, moved[part], 0.0)
+            far_part = window[(h,) + result]
+            err[part] = inc[part] - jnp.where(far_is_ahead, far_part, near_part)
+            grad[part] = mul[part] - jnp.where(far_is_ahead, near_part, far_part) + adj[part]
+        store(err, err_hbm, err_sem, g).start()
+        store(grad, grad_hbm, grad_sem, g).start()
+
+    keep_tangent.wait()
+    for g in range(groups):
+        store(err, err_hbm, err_sem, g).wait()
+        store(grad, grad_hbm, grad_sem, g).wait()
+
 
 def transport_call(sizes, rates, field, side, moved, inc, mul, adj, tangent):
     height, across, levels = inc.shape
-
-    def whole(shape):
-        return pl.BlockSpec(shape[:-1] + (WIDE,), lambda g: (0,) * (len(shape) - 1) + (g,))
-    part = pl.BlockSpec((tangent.shape[0] * WIDE // levels, tangent.shape[1]), lambda g: (g, 0))
-    arrays = (rates, field[None], side[None], moved, inc, mul, adj)
+    anywhere = pl.BlockSpec(memory_space=pl.ANY)
+    arrays = (rates, field[None], side[None], moved, inc, mul, adj, tangent)
     window, state = transport_scratch(inc.shape, sizes[2])
+    dma = pltpu.SemaphoreType.DMA
+    groups = levels // WIDE
     return pl.pallas_call(
         functools.partial(transport_kernel, sizes),
-        grid=(levels // WIDE,),
         out_shape=(jax.ShapeDtypeStruct(inc.shape, F32),) * 2 + (jax.ShapeDtypeStruct(tangent.shape, BF16),),
-        in_specs=[whole(x.shape) for x in arrays] + [part],
-        out_specs=(whole(inc.shape),) * 2 + (part,),
-        scratch_shapes=[window, state, state],
+        in_specs=[anywhere] * len(arrays),
+        out_specs=(anywhere,) * 3,
+        scratch_shapes=[pltpu.VMEM(x.shape, x.dtype) for x in arrays + (inc, inc)] + [
+            window, state, state, dma((groups,)), dma((7,)), dma((groups,)), dma((groups,)), dma],
         compiler_params=pltpu.CompilerParams(vmem_limit_bytes=VMEM_BYTES),
-        cost_estimate=pl.CostEstimate(flops=4 * 17 * height * across * levels, bytes_accessed=16 << 20, transcendentals=0),
+        cost_estimate=pl.CostEstimate(flops=4 * 17 * height * across * levels, bytes_accessed=18 << 20, transcendentals=0),
         name="transport",
-    )(*arrays, tangent)
+    )(*arrays)
 
 
 def local(increment, multiplier, background, obs_cotangent, obs_column, obs_count, transport,

time: 48.5 us -> 49.4 us (1.019)
  Pallas kernels: 47.7 us -> 48.5 us
where the time goes in v6:
time: 49.4 us; the launch traced here: 49.1 us
  Pallas kernels  48.5 us (98%)
  between operations  0.64 us (1%)
    pallas_call x1, Pallas kernels, exchange(): pl.pallas_call(functools.partial(exchange_kernel, sizes), out_shape=(jax....  33.7 us
    pallas_call x1, Pallas kernels, transport_call(): pl.pallas_call(functools.partial(transport_kernel, sizes), out_shape=(jax...  14.8 us

profile of v6, /device:TPU:1, one launch (start us, length us, event | category | flops | bytes accessed | tf_op | source)
XLA Modules:
  0.0 49.1 jit_solution(8310625563390885554)
XLA Ops:
  0.6 33.7 %exchange.1 = (bf16[32,64,512]{2,1,0:T(8,128)(2,1)}, bf16[16,16,512]{2,1,0:T(8,128)(2,1)}, bf16[2048,512]{1,0:T(8,128)(2,1)}, f32[1024,512]{1,0:T(8,128)}, f32[16,64,512]{2,1,0:T(8,128)}) custom-call(s32[8]{0:T(128)} %bitcast.27, s32[16,128]{1,0:T(8,128)} %bitcast.25, f32[16,64,512]{2,1,0:T(8,128)} %bitcast.13, f32[16,64,512]{2,1,0:T(8,128)} %bitcast.15, ...), custom_call_target="tpu_custom_call" | custom-call | flops 9663676416 | bytes 20971520 | tf_op jit(solution)/shard_map/exchange/pallas_call | solution.py:342
  34.3 14.8 %transport.1 = (f32[16,64,512]{2,1,0:T(8,128)}, f32[16,64,512]{2,1,0:T(8,128)}, bf16[2048,512]{1,0:T(8,128)(2,1)}) custom-call(f32[8,512]{1,0:T(8,128)} %rates_hbm.3, bf16[1,32,64,512]{3,2,1,0:T(8,128)(2,1)} %bitcast.17, bf16[1,16,16,512]{3,2,1,0:T(8,128)(2,1)} %bitcast.19, f32[16,64,512]{2,1,0:T(8,128)} %get-tuple-element.13.moved_hbm, ...), custom_call_target="tpu_custom_call" | custom-call | flops 35651584 | bytes 18874368 | tf_op jit(solution)/shard_map/transport/pallas_call | solution.py:540
